TPU v7x, 32 devices: a whole 2x2x4 slice. The times are simulated.
32 devices in a mesh: seastate: 2 (over y), bx: 4 (over z), by: 4 (over x, core).
Axes of the slice: x: 2, y: 2, z: 4, core: 2. Of those that a mesh axis runs over, the one named last changes fastest.
Arguments:
- leaf_factor: bfloat16 [4, 4, 128, 128, 128], P('bx', 'by', 'seastate'), parts along dimension 2, may hold values from -0.5 to 0.5
- class_maps: bfloat16 [16, 128, 128], P('seastate'), parts along dimension 0, may hold values from -1.25 to 1.25
- depth_class: int32 [4, 4, 128], P('bx', None, 'seastate'), parts along dimension 2, may hold values from 0 to 7
- owners: int32 [4, 4, 128, 1], P('bx', 'by', 'seastate'), parts along dimension 2, may hold values from 0 to 3; in each aligned block of 64 rows (0 to 63, 64 to 127, ..., all dimensions but the last counted through in order) at most 24 rows name the same one
- top_in: float32 [4, 4, 32, 256], P('bx', 'by', 'seastate'), parts along dimension 2, may hold values from -6 to 6
Outputs:
- top_out: float32 [4, 4, 32, 256], P('bx', 'by', 'seastate'), parts along dimension 2
- delivered: float32 [4, 4, 4, 48, 128], P('bx', 'by', None, 'seastate'), parts along dimension 3
There are 2 independent parts, one for each index of `seastate`. A program takes and returns all parts, laid end to end along the dimension named above; each array names one. Nothing has to cross between parts.
Inputs may be any that keep to these rules, and one draw needn't show every extreme that they name: `owners`: among the 64 leaves of one device no bx index is named more than 24 times.
All inputs are finite; a program needn't handle non-finite values.
Results may differ from a plain program's by a relative error of at most 0.0003.
Values may be sent and summed in bfloat16 or wider, within the bound.
A program may use at most 128 MiB of HBM per device.

v0:
```python
import jax
import jax.numpy as jnp
from jax import lax
from jax.sharding import PartitionSpec as P

HIGH = lax.Precision.HIGH


def swapped(value, axis):
    pairs = [(source, source ^ 1) for source in range(lax.axis_size(axis))]
    return lax.ppermute(value, axis, pairs)


def product(left, right):
    return jnp.einsum("nij,njk->nik", left, right, precision=HIGH)


def apply_map(matrix, vector):
    return jnp.einsum("nij,nj->ni", matrix, vector, precision=HIGH)


def ordered(parity, mine, other):
    first = jnp.where(parity == 0, mine, other)
    second = jnp.where(parity == 0, other, mine)
    return first, second


def chosen_maps(classes, class_maps):
    levels = class_maps.shape[0]
    onehot = (classes[:, None] == jnp.arange(levels, dtype=jnp.int32)[None, :]).astype(jnp.bfloat16)
    return jnp.einsum(
        "kc,cab->kab", onehot, class_maps, preferred_element_type=jnp.float32
    ).astype(jnp.bfloat16)


def side_of(fields, side, face):
    outer = jnp.where(side == 0, fields[:, : 2 * face], fields[:, 2 * face : 4 * face])
    south = jnp.where(side == 0, fields[:, 4 * face : 5 * face], fields[:, 5 * face : 6 * face])
    north = jnp.where(side == 0, fields[:, 6 * face : 7 * face], fields[:, 7 * face : 8 * face])
    return jnp.concatenate([outer, south, north], axis=1)


def edges(side, outer, inner, south, north):
    west, east = ordered(side, outer, inner)
    return jnp.concatenate([west, east, south, north], axis=1)


def shards(leaf_factor, class_maps, depth_class, owners, top_in):
    factor = leaf_factor[0, 0]
    leaves_here = factor.shape[0]
    face = factor.shape[1] // 4
    half = leaves_here // 2
    quarter = leaves_here // 4
    row = lax.axis_index("by")
    rp = row % 2
    cp = lax.axis_index("bx") % 2
    fields_here = top_in[0, 0]

    got_factor = swapped(lax.dynamic_slice_in_dim(factor, (1 - rp) * half, half, 0), "by")
    got_fields = swapped(side_of(fields_here, 1 - cp, face), "bx")
    mine_factor = lax.dynamic_slice_in_dim(factor, rp * half, half, 0)
    fields = jnp.concatenate(ordered(cp, side_of(fields_here, cp, face), got_fields), axis=0)
    factor_a, factor_b = ordered(rp, mine_factor, got_factor)
    classes = lax.dynamic_slice(depth_class[0], (row - rp, rp * half), (2, half))

    def leaf_maps(own_classes, own_factor):
        chosen = chosen_maps(own_classes, class_maps)
        return jnp.einsum("kab,kbc->kac", chosen, own_factor, preferred_element_type=jnp.float32)

    map_a = leaf_maps(classes[0], factor_a)
    map_b = leaf_maps(classes[1], factor_b)
    nothing = jnp.zeros((half, face), jnp.float32)
    known_a = edges(cp, fields[:, :face], nothing, fields[:, 2 * face : 3 * face], nothing)
    known_b = edges(cp, fields[:, face : 2 * face], nothing, nothing, fields[:, 3 * face :])
    from_a = apply_map(map_a, known_a)
    from_b = apply_map(map_b, known_b)

    def inner_of(value, axis):
        first = lax.slice_in_dim(value, 0, face, axis=axis)
        second = lax.slice_in_dim(value, face, 2 * face, axis=axis)
        return jnp.where(cp == 0, second, first)

    rows_a = map_a[:, 3 * face :]
    rows_b = map_b[:, 2 * face : 3 * face]
    a_ss = rows_a[:, :, 3 * face :]
    b_ss = rows_b[:, :, 2 * face : 3 * face]
    zeros = jnp.zeros((half, face, face), jnp.float32)
    a_si = jnp.concatenate([inner_of(rows_a, 2), zeros, from_a[:, 3 * face :, None]], axis=2)
    b_si = jnp.concatenate(
        [zeros, inner_of(rows_b, 2), from_b[:, 2 * face : 3 * face, None]], axis=2
    )
    both = product(b_ss, jnp.concatenate([a_ss, a_si], axis=2))
    crossed = both[:, :, :face]
    right = both[:, :, face:] - b_si
    inward_a = right + product(crossed, right)
    inward_a = right + product(crossed, inward_a)
    inward_a = right + product(crossed, inward_a)
    inward_b = -a_si - product(a_ss, inward_a)
    inner_a = inner_of(map_a, 1)
    inner_b = inner_of(map_b, 1)
    top_rows = jnp.concatenate(
        [inner_of(inner_a, 2), zeros, inner_of(from_a, 1)[:, :, None]], axis=2
    ) + product(inner_a[:, :, 3 * face :], inward_a)
    low_rows = jnp.concatenate(
        [zeros, inner_of(inner_b, 2), inner_of(from_b, 1)[:, :, None]], axis=2
    ) + product(inner_b[:, :, 2 * face : 3 * face], inward_b)
    level = jnp.concatenate([top_rows, low_rows], axis=1)

    mine_level = lax.dynamic_slice_in_dim(level, cp * quarter, quarter, 0)
    got_level = swapped(lax.dynamic_slice_in_dim(level, (1 - cp) * quarter, quarter, 0), "bx")
    west, east = ordered(cp, mine_level, got_level)
    west_map, west_out = west[:, :, : 2 * face], west[:, :, 2 * face]
    east_map, east_out = east[:, :, : 2 * face], east[:, :, 2 * face]
    start = apply_map(east_map, west_out) - east_out
    inward = start
    for _ in range(3):
        inward = start + apply_map(east_map, apply_map(west_map, inward))
    backward = -west_out - apply_map(west_map, inward)
    kept = jnp.where(cp == 0, inward, backward)
    returned = swapped(jnp.where(cp == 0, backward, inward), "bx")
    inner = jnp.concatenate(ordered(cp, kept, returned), axis=0)

    part_a = apply_map(inward_a[:, :, : 2 * face], inner) + inward_a[:, :, 2 * face]
    part_b = apply_map(inward_b[:, :, : 2 * face], inner) + inward_b[:, :, 2 * face]
    leaf_a = edges(cp, fields[:, :face], inner[:, :face], fields[:, 2 * face : 3 * face], part_a)
    leaf_b = edges(cp, fields[:, face : 2 * face], inner[:, face:], part_b, fields[:, 3 * face :])
    kept_leaves, given_leaves = jnp.where(rp == 0, leaf_a, leaf_b), jnp.where(rp == 0, leaf_b, leaf_a)
    returned_leaves = swapped(given_leaves, "by")
    leaf_fields = jnp.concatenate(ordered(rp, kept_leaves, returned_leaves), axis=0)

    columns = lax.axis_size("bx")
    most = max(2, (3 * leaves_here + 2 * columns - 1) // (2 * columns))
    target = owners[0, 0, :, 0]
    onehot = (target[:, None] == jnp.arange(columns, dtype=jnp.int32)[None, :]).astype(jnp.int32)
    rank = jnp.sum((jnp.cumsum(onehot, axis=0) - onehot) * onehot, axis=1)
    slot = target * most + rank
    selector = (slot[None, :] == jnp.arange(columns * most, dtype=jnp.int32)[:, None]).astype(
        jnp.float32
    )
    outgoing = jnp.dot(selector, leaf_fields, precision=lax.Precision.HIGHEST).reshape(
        columns, most, leaf_fields.shape[1]
    )
    arrived = lax.all_to_all(outgoing, "bx", split_axis=0, concat_axis=0, tiled=True)

    out_a = apply_map(map_a, leaf_a)
    out_b = apply_map(map_b, leaf_b)

    def outer_of(value):
        return jnp.where(cp == 0, value[:, :face], value[:, face : 2 * face])

    out = jnp.concatenate(
        [outer_of(out_a), outer_of(out_b), out_a[:, 2 * face : 3 * face], out_b[:, 3 * face :]],
        axis=1,
    )
    mine_out = lax.dynamic_slice_in_dim(out, cp * quarter, quarter, 0)
    got_out = swapped(lax.dynamic_slice_in_dim(out, (1 - cp) * quarter, quarter, 0), "bx")
    west_out, east_out = ordered(cp, mine_out, got_out)
    top_out = jnp.concatenate(
        [
            west_out[:, : 2 * face],
            east_out[:, : 2 * face],
            west_out[:, 2 * face : 3 * face],
            east_out[:, 2 * face : 3 * face],
            west_out[:, 3 * face :],
            east_out[:, 3 * face :],
        ],
        axis=1,
    )
    return (top_out[None, None], arrived[None, None])


def solution(mesh):
    placed = (
        P("bx", "by", "seastate", None, None),
        P("seastate", None, None),
        P("bx", None, "seastate"),
        P("bx", "by", "seastate", None),
        P("bx", "by", "seastate", None),
    )
    return jax.shard_map(
        shards,
        mesh=mesh,
        in_specs=placed,
        out_specs=(P("bx", "by", "seastate", None), P("bx", "by", None, "seastate", None)),
        check_vma=False,
    )
```

profile of v0, /device:TPU:0, one launch (start us, length us, event | category | flops | bytes accessed | tf_op | source)
XLA Modules:
  0.0 77.5 jit_solution(2444124282203191029)
XLA Ops:
  0.7 1.3 %dynamic-slice_bitcast_fusion = bf16[32,128,128]{2,1,0:T(8,128)(2,1)S(1)} fusion(bf16[1,1,64,128,128]{4,3,2,1,0:T(8,128)(2,1)} %param.5, s32[]{:T(128)S(6)} %select_n.236), kind=kLoop, calls=%fused_computation.21 | loop fusion | bytes 2097156 | tf_op jit(solution)/shard_map/dynamic_slice | solution.py:59
  2.8 2.6 %collective-permute-start.1 = (f32[16,128]{1,0:T(8,128)S(1)}, f32[16,128]{1,0:T(8,128)S(1)}, u32[]{:S(2)}, u32[]{:S(2)}) collective-permute-start(f32[16,128]{1,0:T(8,128)S(1)} %pad_maximum_fusion.9), channel_id=1, source_target_pairs={{0,4},{4,0},{8,12},{12,8},{1,5},{5,1},{9,13},{13,9},{2,6},{6,2},{1... | collective-permute-start | bytes 24584 | tf_op jit(solution)/shard_map/ppermute | solution.py:11
  5.5 1.4 %convolution_convert_fusion.1 = bf16[32,128,128]{2,0,1:T(8,128)(2,1)} fusion(bf16[8,128,128]{2,1,0:T(8,128)(2,1)S(1)} %copy-done, s32[32]{0:T(128)S(1)} %get-tuple-element.50), kind=kOutput, calls=%fused_computation.1 | convolution fusion | flops 8913152 | bytes 1310848 | tf_op jit(solution)/shard_map/kc,cab->kab/dot_general | solution.py:31
  7.7 2.4 %fusion = f32[32,128,128]{2,1,0:T(8,128)S(1)} fusion(bf16[32,128,128]{2,1,0:T(8,128)(2,1)} %collective-permute-done, bf16[32,128,128]{2,0,1:T(8,128)(2,1)} %convolution_convert_fusion.1, pred[]{:T(512)S(6)} %eq.42, bf16[1,1,64,128,128]{4,3,2,1,0:T(8,128)(2,1)} %param.5, s32[]{:T(128)S(6)} %select_n.234), kind=kOutput, calls=%fused_computation.17 | convolution fusion | flops 134742016 | bytes 5242885 | tf_op jit(solution)/shard_map/kab,kbc->kac/dot_general | solution.py:68
  10.2 0.9 %slice_select_fusion.5 = f32[32,32,128]{2,1,0:T(8,128)} fusion(f32[32,128,128]{2,1,0:T(8,128)S(1)} %fusion, pred[]{:T(512)S(6)} %eq.37), kind=kLoop, calls=%fused_computation.55 | loop fusion | flops 131072 | bytes 1572865 | tf_op jit(solution)/shard_map/jit(_where)/select_n | solution.py:81
  11.1 2.0 %fusion.1 = f32[32,128,128]{2,1,0:T(8,128)S(1)} fusion(bf16[32,128,128]{2,1,0:T(8,128)(2,1)} %collective-permute-done, bf16[32,128,128]{2,0,1:T(8,128)(2,1)S(1)} %convolution_convert_fusion, pred[]{:T(512)S(6)} %eq.42, bf16[1,1,64,128,128]{4,3,2,1,0:T(8,128)(2,1)S(1)} %copy-done.9, s32[]{:T(128)S(6)} %select_n.234), kind=kOutput, calls=%fused_computation.18 | convolution fusion | flops 134742016 | bytes 5242885 | tf_op jit(solution)/shard_map/kab,kbc->kac/dot_general | solution.py:68
  13.0 1.7 %fusion.76 = (f32[32,32,32]{2,1,0:T(8,128)}, f32[32,32,32]{2,1,0:T(8,128)S(1)}, f32[32,32,32]{2,1,0:T(8,128)}) fusion(f32[32,128,128]{2,1,0:T(8,128)S(1)} %fusion, pred[]{:T(512)S(6)} %eq.37, f32[32,128,128]{2,1,0:T(8,128)S(1)} %fusion.1), kind=kLoop, calls=%fused_computation.170 | loop fusion | flops 65536 | bytes 1048577 | tf_op jit(solution)/shard_map/slice | solution.py:85
  14.7 1.0 %slice_select_fusion.1 = f32[32,32,128]{2,1,0:T(8,128)} fusion(f32[32,128,128]{2,1,0:T(8,128)S(1)} %fusion.1, pred[]{:T(512)S(6)} %eq.37), kind=kLoop, calls=%fused_computation.48 | loop fusion | flops 131072 | bytes 1572865 | tf_op jit(solution)/shard_map/jit(_where)/select_n | solution.py:81
  15.6 1.7 %fusion.79 = f32[32,1,128]{2,1,0:T(1,128)S(1)} fusion(f32[32,128,128]{2,1,0:T(8,128)S(1)} %fusion, f32[32,128,1]{1,2,0:T(1,128)S(1)} %bitcast.146), kind=kOutput, calls=%fused_computation.173 | convolution fusion | flops 3145728 | bytes 2129920 | tf_op jit(solution)/shard_map/nij,nj->ni/dot_general | solution.py:19
  17.4 1.7 %fusion.80 = f32[32,1,128]{2,1,0:T(1,128)S(1)} fusion(f32[32,128,128]{2,1,0:T(8,128)S(1)} %fusion.1, f32[32,128,1]{1,2,0:T(1,128)S(1)} %bitcast.145), kind=kOutput, calls=%fused_computation.174 | convolution fusion | flops 3145728 | bytes 2129920 | tf_op jit(solution)/shard_map/nij,nj->ni/dot_general | solution.py:19
  19.2 1.1 %copy.173 = f32[32,32,1]{2,1,0:T(8,128)} copy(f32[32,32,1]{1,0,2:T(8,128)S(1)} %get-tuple-element.55) | data formatting | bytes 8192 | tf_op jit(solution)/shard_map/broadcast_in_dim | solution.py:88
  20.3 1.1 %copy.174 = f32[32,32,1]{2,1,0:T(8,128)} copy(f32[32,32,1]{1,0,2:T(8,128)S(1)} %get-tuple-element.32) | data formatting | bytes 8192 | tf_op jit(solution)/shard_map/broadcast_in_dim | solution.py:90
  21.4 2.3 %fusion.21 = f32[32,32,97]{2,1,0:T(8,128)S(1)} fusion(f32[32,128,128]{2,1,0:T(8,128)} %copy-done.1, f32[32,32,1]{2,1,0:T(8,128)} %copy.173, f32[32,32,32]{2,1,0:T(8,128)S(1)} %broadcast_in_dim.29, f32[32,32,32]{2,1,0:T(8,128)S(1)} %get-tuple-element.10, f32[32,32,32]{2,1,0:T(8,128)} %get-tuple-element.9), kind=kOutput, calls=%fused_computation.51 | convolution fusion | flops 19368960 | bytes 2232320 | tf_op jit(solution)/shard_map/nij,njk->nik/dot_general | solution.py:15
  25.8 1.4 %convolution_subtract_fusion = f32[32,32,65]{2,1,0:T(8,128)} fusion(f32[32,32,65]{2,1,0:T(8,128)S(1)} %convolution_add_fusion.3, f32[32,32,32]{2,1,0:T(8,128)S(1)} %broadcast_in_dim.29, f32[32,32,1]{2,1,0:T(8,128)S(1)} %copy-done.12, f32[32,32,32]{2,1,0:T(8,128)S(1)} %copy-done.11, f32[32,128,128]{2,1,0:T(8,128)S(1)} %fusion), kind=kOutput, calls=%fused_computation.8 | convolution fusion | flops 13045760 | bytes 2887680 | tf_op jit(solution)/shard_map/nij,njk->nik/dot_general | solution.py:15
  27.2 1.1 %copy.175 = f32[32,32,1]{2,1,0:T(8,128)} copy(f32[32,32,1]{1,0,2:T(8,128)S(1)} %get-tuple-element.31) | data formatting | bytes 8192 | tf_op jit(solution)/shard_map/broadcast_in_dim | solution.py:105
  28.2 1.1 %copy.170 = f32[32,32,1]{2,1,0:T(8,128)} copy(f32[32,32,1]{1,0,2:T(8,128)S(1)} %get-tuple-element.56) | data formatting | bytes 8192 | tf_op jit(solution)/shard_map/broadcast_in_dim | solution.py:102
  29.3 1.9 %slice_select_fusion = (f32[32,32,32]{2,1,0:T(8,128)S(1)}, f32[32,32,32]{2,1,0:T(8,128)S(1)}) fusion(f32[32,32,128]{2,1,0:T(8,128)} %slice_select_fusion.1, pred[]{:T(512)S(6)} %eq.37, f32[32,32,128]{2,1,0:T(8,128)} %slice_select_fusion.5), kind=kLoop, calls=%fused_computation.47 | loop fusion | flops 65536 | bytes 786433 | tf_op jit(solution)/shard_map/jit(_where)/select_n | solution.py:81
  33.2 0.9 %fusion.15 = f32[16,64,65]{2,1,0:T(8,128)} fusion(s32[]{:T(128)S(6)} %select_n.266, f32[32,32,65]{2,1,0:T(8,128)S(1)} %convolution_add_fusion.2, f32[32,32,65]{2,1,0:T(8,128)S(1)} %convolution_add_fusion.1), kind=kLoop, calls=%fused_computation.37 | loop fusion | flops 66560 | bytes 798724 | tf_op jit(solution)/shard_map/concatenate | solution.py:107
  34.1 1.6 %collective-permute-start.2 = (f32[16,64,65]{2,1,0:T(8,128)}, f32[16,64,65]{2,1,0:T(8,128)S(1)}, u32[]{:S(2)}, u32[]{:S(2)}) collective-permute-start(f32[16,64,65]{2,1,0:T(8,128)} %fusion.15), channel_id=1, source_target_pairs={{0,4},{4,0},{8,12},{12,8},{1,5},{5,1},{9,13},{13,9},{2,6},{6,2},{1... | collective-permute-start | bytes 798728 | tf_op jit(solution)/shard_map/ppermute | solution.py:11
  36.0 1.4 %slice_reduce_fusion = f32[32,32]{1,0:T(8,128)S(1)} fusion(f32[32,32,65]{2,1,0:T(8,128)} %convolution_subtract_fusion), kind=kLoop, calls=%fused_computation.38 | loop fusion | bytes 8192 | tf_op jit(solution)/shard_map/slice | solution.py:124
  37.5 9.9 %collective-permute-done.2 = f32[16,64,65]{2,1,0:T(8,128)S(1)} collective-permute-done((f32[16,64,65]{2,1,0:T(8,128)}, f32[16,64,65]{2,1,0:T(8,128)S(1)}, u32[]{:S(2)}, u32[]{:S(2)}) %collective-permute-start.2) | collective-permute-done | bytes 266272 | tf_op jit(solution)/shard_map/ppermute | solution.py:11
  47.4 1.3 %broadcast_select_fusion.1 = (f32[16,64,65]{2,1,0:T(8,128)S(1)}, f32[16,64,65]{2,1,0:T(8,128)S(1)}) fusion(f32[16,64,65]{2,1,0:T(8,128)S(1)} %collective-permute-done.2, pred[]{:T(512)S(6)} %eq.37, s32[]{:T(128)S(6)} %select_n.267, f32[32,32,65]{2,1,0:T(8,128)} %copy-done.8, f32[32,32,65]{2,1,0:T(8,128)} %copy-done.7), kind=kLoop, calls=%fused_computation.80 | loop fusion | flops 266240 | bytes 1331205 | tf_op jit(solution)/shard_map/jit(_where)/select_n | solution.py:24
  53.9 0.8 %collective-permute-start.3 = (f32[16,64]{1,0:T(8,128)S(1)}, f32[16,64]{1,0:T(8,128)S(1)}, u32[]{:S(2)}, u32[]{:S(2)}) collective-permute-start(f32[16,64]{1,0:T(8,128)S(1)} %broadcast_select_fusion.16), channel_id=1, source_target_pairs={{0,4},{4,0},{8,12},{12,8},{1,5},{5,1},{9,13},{13,9},{2,6},{6,2},{1... | collective-permute-start | bytes 12296 | tf_op jit(solution)/shard_map/ppermute | solution.py:11
  55.1 2.5 %collective-permute-done.3 = f32[16,64]{1,0:T(8,128)S(1)} collective-permute-done((f32[16,64]{1,0:T(8,128)S(1)}, f32[16,64]{1,0:T(8,128)S(1)}, u32[]{:S(2)}, u32[]{:S(2)}) %collective-permute-start.3) | collective-permute-done | bytes 4128 | tf_op jit(solution)/shard_map/ppermute | solution.py:11
  58.9 1.7 %fusion.81 = f32[32,1,128]{2,1,0:T(1,128)S(1)} fusion(f32[32,128,128]{2,1,0:T(8,128)S(1)} %fusion, f32[32,128,1]{1,2,0:T(1,128)S(1)} %bitcast.133), kind=kOutput, calls=%fused_computation.175 | convolution fusion | flops 3145728 | bytes 2129920 | tf_op jit(solution)/shard_map/nij,nj->ni/dot_general | solution.py:19
  60.7 1.7 %fusion.82 = f32[32,1,128]{2,1,0:T(1,128)S(1)} fusion(f32[32,128,128]{2,1,0:T(8,128)S(1)} %copy-done.2, f32[32,128,1]{1,2,0:T(1,128)S(1)} %bitcast.134), kind=kOutput, calls=%fused_computation.176 | convolution fusion | flops 3145728 | bytes 2129920 | tf_op jit(solution)/shard_map/nij,nj->ni/dot_general | solution.py:19
  62.6 0.8 %collective-permute-start.4 = (f32[16,128]{1,0:T(8,128)S(1)}, f32[16,128]{1,0:T(8,128)S(1)}, u32[]{:S(2)}, u32[]{:S(2)}) collective-permute-start(f32[16,128]{1,0:T(8,128)S(1)} %constant_dynamic-slice_fusion), channel_id=1, source_target_pairs={{0,4},{4,0},{8,12},{12,8},{1,5},{5,1},{9,13},{13,9},{2,6},{6,2},{1... | collective-permute-start | bytes 24584 | tf_op jit(solution)/shard_map/ppermute | solution.py:11
  63.4 2.9 %collective-permute-done.4 = f32[16,128]{1,0:T(8,128)S(1)} collective-permute-done((f32[16,128]{1,0:T(8,128)S(1)}, f32[16,128]{1,0:T(8,128)S(1)}, u32[]{:S(2)}, u32[]{:S(2)}) %collective-permute-start.4) | collective-permute-done | bytes 8224 | tf_op jit(solution)/shard_map/ppermute | solution.py:11
  66.4 0.8 %fusion.49 = f32[96,128]{1,0:T(8,128)} fusion(f32[32,128]{1,0:T(8,128)S(1)} %get-tuple-element.14, f32[32,128]{1,0:T(8,128)S(1)} %get-tuple-element.13, s32[64]{0:T(128)S(1)} %multiply_add_fusion), kind=kOutput, calls=%fused_computation.84 | convolution fusion | flops 9451520 | bytes 82176 | tf_op jit(solution)/shard_map/dot_general | solution.py:140
  67.2 4.0 %all-to-all-start = ((f32[4,24,128]{2,1,0:T(8,128)}), f32[4,24,128]{2,1,0:T(8,128)S(1)}, u32[]{:S(2)}, u32[]{:S(2)}) async-start(f32[4,24,128]{2,1,0:T(8,128)} %bitcast.67), calls=%async_computation | async-start | bytes 98304 | tf_op jit(solution)/shard_map/all_to_all | solution.py:143
  71.3 0.7 concatenate.67
  72.0 4.9 %all-to-all-done = f32[4,24,128]{2,1,0:T(8,128)S(1)} async-done(((f32[4,24,128]{2,1,0:T(8,128)}), f32[4,24,128]{2,1,0:T(8,128)S(1)}, u32[]{:S(2)}, u32[]{:S(2)}) %all-to-all-start) | async-done | bytes 49184 | tf_op jit(solution)/shard_map/all_to_all | solution.py:143
  (102 shorter events, 13.8 us)
Async XLA Ops:
  0.6 4.8 %copy-start = (bf16[8,128,128]{2,1,0:T(8,128)(2,1)S(1)}, bf16[8,128,128]{2,1,0:T(8,128)(2,1)}, u32[]{:S(2)}) copy-start(bf16[8,128,128]{2,1,0:T(8,128)(2,1)} %param.6) | copy-start | bytes 786436
  0.6 1.9 %copy-start.17 = (f32[1,1,16,256]{3,2,1,0:T(8,128)S(1)}, f32[1,1,16,256]{3,2,1,0:T(8,128)}, u32[]{:S(2)}) copy-start(f32[1,1,16,256]{3,2,1,0:T(8,128)} %param.9) | copy-start | bytes 49156
  0.7 4.7 %copy-start.19 = (s32[1,4,64]{2,1,0:T(4,128)S(1)}, s32[1,4,64]{2,1,0:T(4,128)}, u32[]{:S(2)}) copy-start(s32[1,4,64]{2,1,0:T(4,128)} %param.7) | copy-start | bytes 3076
  2.0 5.7 %collective-permute-start = (bf16[32,128,128]{2,1,0:T(8,128)(2,1)S(1)}, bf16[32,128,128]{2,1,0:T(8,128)(2,1)}, u32[]{:S(2)}, u32[]{:S(2)}) collective-permute-start(bf16[32,128,128]{2,1,0:T(8,128)(2,1)S(1)} %dynamic-slice_bitcast_fusion), channel_id=1, source_target_pairs={{0,1},{1,0},{2,3},{3,2},{4,5},{5,4},{6,7},{7,6},{8,9},{9,8},{10,11... | collective-permute-start | bytes 3145736 | tf_op jit(solution)/shard_map/ppermute | solution.py:11
  2.8 4.7 %collective-permute-start.1 = (f32[16,128]{1,0:T(8,128)S(1)}, f32[16,128]{1,0:T(8,128)S(1)}, u32[]{:S(2)}, u32[]{:S(2)}) collective-permute-start(f32[16,128]{1,0:T(8,128)S(1)} %pad_maximum_fusion.9), channel_id=1, source_target_pairs={{0,4},{4,0},{8,12},{12,8},{1,5},{5,1},{9,13},{13,9},{2,6},{6,2},{1... | collective-permute-start | bytes 24584 | tf_op jit(solution)/shard_map/ppermute | solution.py:11
  7.7 3.3 %copy-start.9 = (bf16[1,1,64,128,128]{4,3,2,1,0:T(8,128)(2,1)S(1)}, bf16[1,1,64,128,128]{4,3,2,1,0:T(8,128)(2,1)}, u32[]{:S(2)}) copy-start(bf16[1,1,64,128,128]{4,3,2,1,0:T(8,128)(2,1)} %param.5) | copy-start | bytes 6291460
  13.0 4.3 %copy-start.1 = (f32[32,128,128]{2,1,0:T(8,128)}, f32[32,128,128]{2,1,0:T(8,128)S(1)}, u32[]{:S(2)}) copy-start(f32[32,128,128]{2,1,0:T(8,128)S(1)} %fusion.1) | copy-start | bytes 6291460
  14.7 6.7 %copy-start.10 = (f32[32,32,32]{2,1,0:T(8,128)}, f32[32,32,32]{2,1,0:T(8,128)S(1)}, u32[]{:S(2)}) copy-start(f32[32,32,32]{2,1,0:T(8,128)S(1)} %get-tuple-element.10) | copy-start | bytes 393220
  21.3 2.4 %copy-start.13 = (f32[32,32,32]{2,1,0:T(8,128)S(1)}, f32[32,32,32]{2,1,0:T(8,128)}, u32[]{:S(2)}) copy-start(f32[32,32,32]{2,1,0:T(8,128)} %get-tuple-element.54) | copy-start | bytes 393220
  21.3 2.4 %copy-start.14 = (f32[32,32,1]{2,1,0:T(8,128)S(1)}, f32[32,32,1]{2,1,0:T(8,128)}, u32[]{:S(2)}) copy-start(f32[32,32,1]{2,1,0:T(8,128)} %copy.174) | copy-start | bytes 12292
  24.6 1.0 %copy-start.11 = (f32[32,32,32]{2,1,0:T(8,128)S(1)}, f32[32,32,32]{2,1,0:T(8,128)}, u32[]{:S(2)}) copy-start(f32[32,32,32]{2,1,0:T(8,128)} %copy-done.10) | copy-start | bytes 393220
  24.6 1.2 %copy-start.12 = (f32[32,32,1]{2,1,0:T(8,128)S(1)}, f32[32,32,1]{2,1,0:T(8,128)}, u32[]{:S(2)}) copy-start(f32[32,32,1]{2,1,0:T(8,128)} %copy.173) | copy-start | bytes 12292
  29.3 2.0 %copy-start.3 = (f32[32,32,128]{2,1,0:T(8,128)S(1)}, f32[32,32,128]{2,1,0:T(8,128)}, u32[]{:S(2)}) copy-start(f32[32,32,128]{2,1,0:T(8,128)} %slice_select_fusion.5) | copy-start | bytes 1572868
  29.3 2.0 %copy-start.16 = (f32[32,32,1]{2,1,0:T(8,128)S(1)}, f32[32,32,1]{2,1,0:T(8,128)}, u32[]{:S(2)}) copy-start(f32[32,32,1]{2,1,0:T(8,128)} %copy.170) | copy-start | bytes 12292
  31.3 1.0 %copy-start.4 = (f32[32,32,128]{2,1,0:T(8,128)S(1)}, f32[32,32,128]{2,1,0:T(8,128)}, u32[]{:S(2)}) copy-start(f32[32,32,128]{2,1,0:T(8,128)} %slice_select_fusion.1) | copy-start | bytes 1572868
  31.3 1.2 %copy-start.5 = (f32[32,32,65]{2,1,0:T(8,128)S(1)}, f32[32,32,65]{2,1,0:T(8,128)}, u32[]{:S(2)}) copy-start(f32[32,32,65]{2,1,0:T(8,128)} %convolution_subtract_fusion) | copy-start | bytes 798724
  31.3 1.3 %copy-start.15 = (f32[32,32,1]{2,1,0:T(8,128)S(1)}, f32[32,32,1]{2,1,0:T(8,128)}, u32[]{:S(2)}) copy-start(f32[32,32,1]{2,1,0:T(8,128)} %copy.175) | copy-start | bytes 12292
  31.9 2.2 %copy-start.7 = (f32[32,32,65]{2,1,0:T(8,128)}, f32[32,32,65]{2,1,0:T(8,128)S(1)}, u32[]{:S(2)}) copy-start(f32[32,32,65]{2,1,0:T(8,128)S(1)} %convolution_add_fusion.2) | copy-start | bytes 798724
  32.6 3.1 %copy-start.18 = (s32[1,1,64,1]{2,3,1,0:T(1,128)S(1)}, s32[1,1,64,1]{2,3,1,0:T(1,128)}, u32[]{:S(2)}) copy-start(s32[1,1,64,1]{2,3,1,0:T(1,128)} %param.8) | copy-start | bytes 772
  33.2 2.5 %copy-start.8 = (f32[32,32,65]{2,1,0:T(8,128)}, f32[32,32,65]{2,1,0:T(8,128)S(1)}, u32[]{:S(2)}) copy-start(f32[32,32,65]{2,1,0:T(8,128)S(1)} %convolution_add_fusion.1) | copy-start | bytes 798724
  34.1 13.3 %collective-permute-start.2 = (f32[16,64,65]{2,1,0:T(8,128)}, f32[16,64,65]{2,1,0:T(8,128)S(1)}, u32[]{:S(2)}, u32[]{:S(2)}) collective-permute-start(f32[16,64,65]{2,1,0:T(8,128)} %fusion.15), channel_id=1, source_target_pairs={{0,4},{4,0},{8,12},{12,8},{1,5},{5,1},{9,13},{13,9},{2,6},{6,2},{1... | collective-permute-start | bytes 798728 | tf_op jit(solution)/shard_map/ppermute | solution.py:11
  50.7 7.0 %copy-start.6 = (f32[32,32,65]{2,1,0:T(8,128)S(1)}, f32[32,32,65]{2,1,0:T(8,128)}, u32[]{:S(2)}) copy-start(f32[32,32,65]{2,1,0:T(8,128)} %convolution_subtract_fusion) | copy-start | bytes 798724
  53.9 6.8 %copy-start.2 = (f32[32,128,128]{2,1,0:T(8,128)S(1)}, f32[32,128,128]{2,1,0:T(8,128)}, u32[]{:S(2)}) copy-start(f32[32,128,128]{2,1,0:T(8,128)} %copy-done.1) | copy-start | bytes 6291460
  53.9 3.7 %collective-permute-start.3 = (f32[16,64]{1,0:T(8,128)S(1)}, f32[16,64]{1,0:T(8,128)S(1)}, u32[]{:S(2)}, u32[]{:S(2)}) collective-permute-start(f32[16,64]{1,0:T(8,128)S(1)} %broadcast_select_fusion.16), channel_id=1, source_target_pairs={{0,4},{4,0},{8,12},{12,8},{1,5},{5,1},{9,13},{13,9},{2,6},{6,2},{1... | collective-permute-start | bytes 12296 | tf_op jit(solution)/shard_map/ppermute | solution.py:11
  62.6 3.7 %collective-permute-start.4 = (f32[16,128]{1,0:T(8,128)S(1)}, f32[16,128]{1,0:T(8,128)S(1)}, u32[]{:S(2)}, u32[]{:S(2)}) collective-permute-start(f32[16,128]{1,0:T(8,128)S(1)} %constant_dynamic-slice_fusion), channel_id=1, source_target_pairs={{0,4},{4,0},{8,12},{12,8},{1,5},{5,1},{9,13},{13,9},{2,6},{6,2},{1... | collective-permute-start | bytes 24584 | tf_op jit(solution)/shard_map/ppermute | solution.py:11
  63.4 3.0 %collective-permute-start.5 = (f32[32,128]{1,0:T(8,128)S(1)}, f32[32,128]{1,0:T(8,128)S(1)}, u32[]{:S(2)}, u32[]{:S(2)}) collective-permute-start(f32[32,128]{1,0:T(8,128)S(1)} %get-tuple-element.2), channel_id=1, source_target_pairs={{0,1},{1,0},{2,3},{3,2},{4,5},{5,4},{6,7},{7,6},{8,9},{9,8},{10,11... | collective-permute-start | bytes 49160 | tf_op jit(solution)/shard_map/ppermute | solution.py:11
  67.2 9.7 %all-to-all-start = ((f32[4,24,128]{2,1,0:T(8,128)}), f32[4,24,128]{2,1,0:T(8,128)S(1)}, u32[]{:S(2)}, u32[]{:S(2)}) async-start(f32[4,24,128]{2,1,0:T(8,128)} %bitcast.67), calls=%async_computation | async-start | bytes 98304 | tf_op jit(solution)/shard_map/all_to_all | solution.py:143
where the time goes:
time: 78 us; the launch traced here: 77.5 us
  matrix products  25.3 us (32%)
  waiting for transfers between devices  20.3 us (26%)
  local copies, waits for them, and re-layouts  11 us (14%)
  starting transfers between devices  10.4 us (13%)
  other arithmetic  9.55 us (12%)
  between operations  1.01 us (1%)
    ppermute x6, waiting for transfers between devices, swapped(): return lax.ppermute(value, axis, pairs)  15.4 us
    dot_general x14, matrix products, apply_map(): return jnp.einsum('nij,nj->ni', matrix, vector, precision=HIGH)  12.3 us
    ppermute x6, starting transfers between devices, swapped(): return lax.ppermute(value, axis, pairs)  6.36 us
    dot_general x7, matrix products, product(): return jnp.einsum('nij,njk->nik', left, right, precision=HIGH)  5.84 us
    all_to_all x1, waiting for transfers between devices, shards(): lax.all_to_all(outgoing, 'bx', split_axis=0, concat_axis=0, tiled=True)  4.94 us
    dot_general x2, matrix products, leaf_maps(): jnp.einsum('kab,kbc->kac', chosen, own_factor, preferred_element_type=jnp...  4.39 us
    all_to_all x1, starting transfers between devices, shards(): lax.all_to_all(outgoing, 'bx', split_axis=0, concat_axis=0, tiled=True)  4.03 us
    select_n x3, other arithmetic, inner_of(): return jnp.where(cp == 0, second, first)  3.79 us
  transfers between devices with their start and end apart: 7, of which 4 were waited for; matrix products, arithmetic and copies ran while one was open for 7% of the time, Pallas kernels for 0%

commit v1 on v0

v1 whole, which is shorter than its diff:
```python
import functools

import jax
import jax.numpy as jnp
from jax import lax
from jax.experimental import pallas as pl
from jax.experimental.pallas import tpu as pltpu
from jax.sharding import PartitionSpec as P

MESH = pl.DeviceIdType.MESH
F32 = jnp.float32
BF16 = jnp.bfloat16


def halves(value):
    high = value.astype(BF16)
    return high, (value - high.astype(F32)).astype(BF16)


def product(left, right):
    left_high, left_low = halves(left)
    right_high, right_low = halves(right)
    return jnp.dot(
        jnp.concatenate([left_high, left_high, left_low], axis=1),
        jnp.concatenate([right_high, right_low, right_high], axis=0),
        preferred_element_type=F32,
    )


def kernel(
    columns,
    most,
    classes_ref,
    factor_ref,
    maps_ref,
    owners_ref,
    top_ref,
    out_ref,
    delivered_ref,
    factors,
    leaf_maps,
    inward,
    blocks,
    answers,
    fields,
    fields_out,
    transposed,
    opened,
    inner,
    inner_out,
    leaves,
    home,
    outgoing,
    arrived,
    outs,
    outs_out,
    local_sem,
    factor_send,
    factor_recv,
    field_sem,
    block_send,
    block_recv,
    answer_sem,
    inner_sem,
    leaf_sem,
    outs_sem,
    all_send,
    all_recv,
):
    leaves_here, leaf = factor_ref.shape[0], factor_ref.shape[1]
    face = leaf // 4
    half, quarter = leaves_here // 2, leaves_here // 4
    pairs = quarter // 2
    row, column = lax.axis_index("by"), lax.axis_index("bx")
    rp, cp = lax.rem(row, 2), lax.rem(column, 2)
    row_mate, column_mate = row + 1 - 2 * rp, column + 1 - 2 * cp
    first, second = (1 - cp) * quarter, cp * quarter
    west = cp == 0

    def to_row_mate(source, target, send, recv):
        return pltpu.make_async_remote_copy(
            src_ref=source, dst_ref=target, send_sem=send, recv_sem=recv,
            device_id={"by": row_mate}, device_id_type=MESH,
        )

    def to_column_mate(source, target, send, recv):
        return pltpu.make_async_remote_copy(
            src_ref=source, dst_ref=target, send_sem=send, recv_sem=recv,
            device_id={"bx": column_mate}, device_id_type=MESH,
        )

    own_copies, mate_copies = [], []
    for index, begin in enumerate((first, second)):
        own = pltpu.make_async_copy(
            factor_ref.at[pl.ds(rp * half + begin, quarter)],
            factors.at[rp, pl.ds(begin, quarter)],
            local_sem.at[index],
        )
        own.start()
        own_copies.append(own)
        mate_copies.append(
            to_row_mate(
                factor_ref.at[pl.ds((1 - rp) * half + begin, quarter)],
                factors.at[rp, pl.ds(begin, quarter)],
                factor_send.at[index],
                factor_recv.at[index],
            )
        )

    barrier = pltpu.get_barrier_semaphore()
    pl.semaphore_signal(barrier, inc=1, device_id={"by": row_mate}, device_id_type=MESH)
    for step in range(1, columns):
        pl.semaphore_signal(
            barrier, inc=1, device_id={"bx": lax.rem(column + step, columns)}, device_id_type=MESH
        )
    pl.semaphore_wait(barrier, columns)
    for copy in mate_copies:
        copy.start()

    top = top_ref[...]
    none = jnp.zeros((quarter, face), F32)

    def part(index):
        return top[:, index * face : (index + 1) * face]

    def row_of(*parts):
        return jnp.concatenate(parts, axis=1)

    sides = (
        (row_of(part(0), none, part(4), none), row_of(part(1), none, none, part(6))),
        (row_of(none, part(2), part(5), none), row_of(none, part(3), none, part(7))),
    )
    for index in range(2):
        mine = jnp.where(west, sides[0][index], sides[1][index])
        other = jnp.where(west, sides[1][index], sides[0][index])
        for box in range(quarter):
            fields[cp, index, box] = mine[box : box + 1]
            fields_out[index, box] = other[box : box + 1]
    field_copy = to_column_mate(fields_out, fields.at[cp], field_sem.at[0], field_sem.at[1])
    field_copy.start()

    sub_face = lax.broadcasted_iota(jnp.int32, (face, face), 0)
    lane_face = lax.broadcasted_iota(jnp.int32, (face, face), 1)
    identity = (sub_face == lane_face).astype(F32)
    sub_two = lax.broadcasted_iota(jnp.int32, (2 * face, leaf), 0)
    lane_two = lax.broadcasted_iota(jnp.int32, (2 * face, leaf), 1)
    no_map = jnp.zeros((face, leaf), F32)

    def block_copy(step):
        return to_column_mate(
            blocks.at[0, pl.ds(2 * step, 2)],
            blocks.at[1 + cp, pl.ds(2 * step, 2)],
            block_send.at[step],
            block_recv.at[step],
        )

    def inner_rows(matrix):
        return jnp.where(west, matrix[face : 2 * face], matrix[:face])

    def upward(turn, carry):
        stage, step = turn // 4, lax.rem(turn, 4)
        side = jnp.where(turn < 4, 1 - cp, cp)

        @pl.when(step == 0)
        def _():
            @pl.when(stage == 0)
            def _():
                own_copies[0].wait()
                mate_copies[0].wait_recv()
                field_copy.wait_recv()

            @pl.when(stage == 1)
            def _():
                own_copies[1].wait()
                mate_copies[1].wait_recv()

        slot = jnp.where(turn < 4, 0, 1 + cp)
        boxes = [2 * step, 2 * step + 1, 2 * step + pairs, 2 * step + 1 + pairs]
        places = [side * quarter + box for box in boxes]
        maps_a, maps_b = [], []
        for place in places:
            class_a = classes_ref[row - rp, rp * half + place]
            class_b = classes_ref[row - rp + 1, rp * half + place]
            map_a = jnp.dot(maps_ref[class_a], factors[0, place], preferred_element_type=F32)
            map_b = jnp.dot(maps_ref[class_b], factors[1, place], preferred_element_type=F32)
            leaf_maps[0, place] = map_a
            leaf_maps[1, place] = map_b
            maps_a.append(map_a)
            maps_b.append(map_b)
        rows_a = [m[3 * face :] for m in maps_a]
        rows_b = [m[2 * face : 3 * face] for m in maps_b]
        a_ss = [m[:, 3 * face :] for m in rows_a]
        b_ss = [m[:, 2 * face : 3 * face] for m in rows_b]
        crossed_rows = [product(b, a) for b, a in zip(b_ss, rows_a)]
        crossed = [m[:, 3 * face :] for m in crossed_rows]
        squares = [product(m, m) for m in crossed]
        inverses = [product(identity + m, identity + s) for m, s in zip(crossed, squares)]
        inward_a = [
            product(w, jnp.concatenate([c, -b], axis=1))
            for w, c, b in zip(inverses, crossed_rows, rows_b)
        ]
        inner_a = [inner_rows(m) for m in maps_a]
        inner_b = [inner_rows(m) for m in maps_b]
        spread = [
            product(jnp.concatenate([s, i[:, 3 * face :]], axis=0), x)
            for s, i, x in zip(a_ss, inner_a, inward_a)
        ]
        inward_b = [
            -jnp.concatenate([a, no_map], axis=1) - s[:face] for a, s in zip(rows_a, spread)
        ]
        upper = [
            jnp.concatenate([i, no_map], axis=1) + s[face:] for i, s in zip(inner_a, spread)
        ]
        lower = [
            jnp.concatenate([no_map, i], axis=1) + product(i[:, 2 * face : 3 * face], y)
            for i, y in zip(inner_b, inward_b)
        ]
        packed = []
        for index, (box, place) in enumerate(zip(boxes, places)):
            inward[place, :face] = inward_a[index]
            inward[place, face:] = inward_b[index]
            level = jnp.concatenate([upper[index], lower[index]], axis=0)
            field_a, field_b = fields[side, 0, box], fields[side, 1, box]
            answer = jnp.sum(
                level[:, :leaf] * field_a + level[:, leaf:] * field_b, axis=1, keepdims=True
            )
            answers[slot, box] = jnp.sum(
                jnp.where(sub_two == lane_two, answer, 0.0), axis=0, keepdims=True
            )
            offset = 2 * face * (index // 2)
            shift = offset - face * (1 - cp) + leaf
            moved_a = pltpu.roll(level[:, :leaf], lax.rem(shift, leaf), 1)
            moved_b = pltpu.roll(level[:, leaf:], lax.rem(shift + face, leaf), 1)
            packed.append(jnp.where(lane_two < offset + face, moved_a, moved_b))
        for index in range(2):
            blocks[slot, 2 * step + index] = jnp.where(
                lane_two < 2 * face, packed[index], packed[index + 2]
            )

        @pl.when(stage == 0)
        def _():
            block_copy(step).start()

        return carry

    lax.fori_loop(0, 8, upward, 0)
    answer_copy = to_column_mate(
        answers.at[0], answers.at[1 + cp], answer_sem.at[0], answer_sem.at[1]
    )
    answer_copy.start()

    target = owners_ref[...]
    named = (lax.broadcasted_iota(jnp.int32, (columns, leaves_here), 0) == target).astype(F32)
    before = lax.broadcasted_iota(jnp.int32, (leaves_here, leaves_here), 0) < (
        lax.broadcasted_iota(jnp.int32, (leaves_here, leaves_here), 1)
    )
    earlier = jnp.dot(
        named.astype(BF16), before.astype(F32).astype(BF16), preferred_element_type=F32
    )
    rank = jnp.sum(named * earlier, axis=0, keepdims=True)
    slots = target.astype(F32) * most + rank
    wanted = lax.broadcasted_iota(jnp.int32, (columns * most, leaves_here), 0).astype(F32)
    selector = (wanted == slots).astype(F32).astype(BF16)

    for step in range(4):
        block_copy(step).wait_recv()
    answer_copy.wait_recv()
    for index in range(pairs):
        both = blocks[1, index].T
        transposed[index] = both[: 2 * face]
        transposed[index + pairs] = both[2 * face :]
        other = blocks[2, index]
        opened[index] = other[:, : 2 * face]
        opened[index + pairs] = other[:, 2 * face :]
    diagonal = (
        lax.broadcasted_iota(jnp.int32, (quarter, 2 * face, 2 * face), 1)
        == lax.broadcasted_iota(jnp.int32, (quarter, 2 * face, 2 * face), 2)
    )
    west_out = answers[1][:, :, : 2 * face]
    east_out = answers[2][:, :, : 2 * face]
    start = jnp.sum(
        opened[...] * west_out - jnp.where(diagonal, east_out, 0.0), axis=2, keepdims=True
    )
    value = start
    for _ in range(3):
        between = jnp.sum(transposed[...] * value, axis=1, keepdims=True)
        value = start + jnp.sum(opened[...] * between, axis=2, keepdims=True)
    to_west = jnp.sum(jnp.where(diagonal, value, 0.0), axis=1, keepdims=True)
    to_east = -west_out - jnp.sum(transposed[...] * value, axis=1, keepdims=True)
    gap = jnp.zeros((quarter, 1, face), F32)
    gaps = jnp.zeros((quarter, 1, 2 * face), F32)
    west_rows = (
        jnp.concatenate([gap, to_west[:, :, :face], gaps], axis=2),
        jnp.concatenate([gap, to_west[:, :, face:], gaps], axis=2),
    )
    east_rows = (
        jnp.concatenate([to_east[:, :, :face], gap, gaps], axis=2),
        jnp.concatenate([to_east[:, :, face:], gap, gaps], axis=2),
    )
    for index in range(2):
        inner[cp, index] = jnp.where(west, west_rows[index], east_rows[index])
        inner_out[index] = jnp.where(west, east_rows[index], west_rows[index])
    inner_copy = to_column_mate(inner_out, inner.at[cp], inner_sem.at[0], inner_sem.at[1])
    inner_copy.start()

    sub_row = lax.broadcasted_iota(jnp.int32, (face, leaf), 0)
    lane_row = lax.broadcasted_iota(jnp.int32, (face, leaf), 1)

    def downward(turn, carry):
        side = jnp.where(turn < 4, cp, 1 - cp)

        @pl.when(turn == 4)
        def _():
            inner_copy.wait_recv()

        for index in range(4):
            box = lax.rem(turn, 4) * 4 + index
            place = side * quarter + box
            field_a = fields[side, 0, box] + inner[side, 0, box]
            field_b = fields[side, 1, box] + inner[side, 1, box]
            both = inward[place]
            found = jnp.sum(
                both[:, :leaf] * field_a + both[:, leaf:] * field_b, axis=1, keepdims=True
            )
            north = jnp.where(lane_row == sub_row + 3 * face, found[:face], 0.0)
            south = jnp.where(lane_row == sub_row + 2 * face, found[face:], 0.0)
            leaves[0, pl.ds(place, 1)] = field_a + jnp.sum(north, axis=0, keepdims=True)
            leaves[1, pl.ds(place, 1)] = field_b + jnp.sum(south, axis=0, keepdims=True)
        return carry

    lax.fori_loop(0, 8, downward, 0)
    leaf_copy = to_row_mate(leaves.at[1 - rp], home.at[rp], leaf_sem.at[0], leaf_sem.at[1])
    leaf_copy.start()
    home[rp] = leaves[rp]

    sub_all = lax.broadcasted_iota(jnp.int32, (leaf, leaf), 0)
    lane_all = lax.broadcasted_iota(jnp.int32, (leaf, leaf), 1)

    def outward(side, target_ref):
        def body(turn, carry):
            for index in range(4):
                box = turn * 4 + index
                place = side * quarter + box
                leaf_a = leaves[0, pl.ds(place, 1)]
                leaf_b = leaves[1, pl.ds(place, 1)]
                outer = pl.ds(cp * face, face)
                found = jnp.concatenate(
                    [
                        leaf_maps[0, place, outer] * leaf_a,
                        leaf_maps[1, place, outer] * leaf_b,
                        leaf_maps[0, place, 2 * face : 3 * face] * leaf_a,
                        leaf_maps[1, place, 3 * face :] * leaf_b,
                    ],
                    axis=0,
                )
                found = jnp.sum(found, axis=1, keepdims=True)
                target_ref[pl.ds(box, 1)] = jnp.sum(
                    jnp.where(sub_all == lane_all, found, 0.0), axis=0, keepdims=True
                )
            return carry

        lax.fori_loop(0, quarter // 4, body, 0)

    outward(1 - cp, outs_out)
    outs_copy = to_column_mate(outs_out, outs.at[cp], outs_sem.at[0], outs_sem.at[1])
    outs_copy.start()

    leaf_copy.wait_recv()
    values = jnp.concatenate([home[0], home[1]], axis=0)
    high, rest = halves(values)
    middle, low = halves(values - high.astype(F32))
    chosen = (
        jnp.dot(selector, high, preferred_element_type=F32)
        + jnp.dot(selector, middle, preferred_element_type=F32)
        + jnp.dot(selector, low, preferred_element_type=F32)
    )
    for owner in range(columns):
        outgoing[owner] = chosen[owner * most : (owner + 1) * most]
    all_copies = []
    for step in range(1, columns):
        owner = lax.rem(column + step, columns)
        copy = pltpu.make_async_remote_copy(
            src_ref=outgoing.at[owner],
            dst_ref=arrived.at[column],
            send_sem=all_send.at[step - 1],
            recv_sem=all_recv.at[step - 1],
            device_id={"bx": owner},
            device_id_type=MESH,
        )
        copy.start()
        all_copies.append(copy)
    arrived[column] = outgoing[column]

    outward(cp, outs.at[cp])
    outs_copy.wait_recv()
    out_west, out_east = outs[0], outs[1]
    out_ref[...] = jnp.concatenate(
        [
            out_west[:, : 2 * face],
            out_east[:, : 2 * face],
            out_west[:, 2 * face : 3 * face],
            out_east[:, 2 * face : 3 * face],
            out_west[:, 3 * face :],
            out_east[:, 3 * face :],
        ],
        axis=1,
    )
    for copy in all_copies:
        copy.wait_recv()
    delivered_ref[...] = arrived[...]

    for copy in mate_copies + all_copies:
        copy.wait_send()
    for copy in (field_copy, answer_copy, inner_copy, leaf_copy, outs_copy):
        copy.wait_send()
    for step in range(4):
        block_copy(step).wait_send()


def shards(leaf_factor, class_maps, depth_class, owners, top_in):
    factor = leaf_factor[0, 0]
    leaves_here, leaf = factor.shape[0], factor.shape[1]
    half, quarter = leaves_here // 2, leaves_here // 4
    inside = leaf // 2
    columns = lax.axis_size("bx")
    most = max(2, (3 * leaves_here + 2 * columns - 1) // (2 * columns))
    whole = pl.BlockSpec(memory_space=pltpu.VMEM)
    top_out, arrived = pl.pallas_call(
        functools.partial(kernel, columns, most),
        out_shape=(
            jax.ShapeDtypeStruct((quarter, 2 * leaf), F32),
            jax.ShapeDtypeStruct((columns, most, leaf), F32),
        ),
        in_specs=[
            pl.BlockSpec(memory_space=pltpu.SMEM),
            pl.BlockSpec(memory_space=pl.ANY),
            whole,
            whole,
            whole,
        ],
        out_specs=(whole, whole),
        scratch_shapes=[
            pltpu.VMEM((2, half, leaf, leaf), BF16),
            pltpu.VMEM((2, half, leaf, leaf), F32),
            pltpu.VMEM((half, inside, 2 * leaf), F32),
            pltpu.VMEM((3, quarter // 2, inside, leaf), F32),
            pltpu.VMEM((3, quarter, 1, leaf), F32),
            pltpu.VMEM((2, 2, quarter, 1, leaf), F32),
            pltpu.VMEM((2, quarter, 1, leaf), F32),
            pltpu.VMEM((quarter, inside, inside), F32),
            pltpu.VMEM((quarter, inside, inside), F32),
            pltpu.VMEM((2, 2, quarter, 1, leaf), F32),
            pltpu.VMEM((2, quarter, 1, leaf), F32),
            pltpu.VMEM((2, half, leaf), F32),
            pltpu.VMEM((2, half, leaf), F32),
            pltpu.VMEM((columns, most, leaf), F32),
            pltpu.VMEM((columns, most, leaf), F32),
            pltpu.VMEM((2, quarter, leaf), F32),
            pltpu.VMEM((quarter, leaf), F32),
            pltpu.SemaphoreType.DMA((2,)),
            pltpu.SemaphoreType.DMA((2,)),
            pltpu.SemaphoreType.DMA((2,)),
            pltpu.SemaphoreType.DMA((2,)),
            pltpu.SemaphoreType.DMA((4,)),
            pltpu.SemaphoreType.DMA((4,)),
            pltpu.SemaphoreType.DMA((2,)),
            pltpu.SemaphoreType.DMA((2,)),
            pltpu.SemaphoreType.DMA((2,)),
            pltpu.SemaphoreType.DMA((2,)),
            pltpu.SemaphoreType.DMA((columns - 1,)),
            pltpu.SemaphoreType.DMA((columns - 1,)),
        ],
        compiler_params=pltpu.CompilerParams(
            collective_id=0, has_side_effects=True, vmem_limit_bytes=40 * 1024 * 1024
        ),
    )(depth_class[0], factor, class_maps, owners[0, 0].reshape(1, leaves_here), top_in[0, 0])
    return (top_out[None, None], arrived[None, None])


def solution(mesh):
    placed = (
        P("bx", "by", "seastate", None, None),
        P("seastate", None, None),
        P("bx", None, "seastate"),
        P("bx", "by", "seastate", None),
        P("bx", "by", "seastate", None),
    )
    return jax.shard_map(
        shards,
        mesh=mesh,
        in_specs=placed,
        out_specs=(P("bx", "by", "seastate", None), P("bx", "by", None, "seastate", None)),
        check_vma=False,
    )
```

time: 78 us -> 38.8 us (0.50)
  Pallas kernels: 0 us -> 32.1 us
  matrix products: 25.3 us -> 0 us
  waiting for transfers between devices: 20.3 us -> 0 us
  starting transfers between devices: 10.4 us -> 0 us
  other arithmetic: 9.55 us -> 0 us
  local copies, waits for them, and re-layouts: 11 us -> 5.81 us
    pallas_call x0 -> x1, Pallas kernels: none -> 32.1 us  [shards(): pl.pallas_call(functools.partial(kernel, columns, most), out_shape=(jax.S...]
    dot_general x26 -> x0, matrix products: 25.3 us -> none  [the longest x14 12.3 us: apply_map(): return jnp.einsum('nij,nj->ni', matrix, vector, precision=HIGH)]
    ppermute x6 -> x0, waiting for transfers between devices: 15.4 us -> none  [swapped(): return lax.ppermute(value, axis, pairs)]
    ppermute x6 -> x0, starting transfers between devices: 6.36 us -> none  [swapped(): return lax.ppermute(value, axis, pairs)]
    select_n x18 -> x0, other arithmetic: 5.75 us -> none  [the longest x3 3.79 us: inner_of(): return jnp.where(cp == 0, second, first)]
    all_to_all x1 -> x0, waiting for transfers between devices: 4.94 us -> none  [shards(): lax.all_to_all(outgoing, 'bx', split_axis=0, concat_axis=0, tiled=True)]
    broadcast_in_dim x6 -> x0, local copies, waits for them, and re-layouts: 4.32 us -> none  [the longest x1 1.08 us: shards(): inner_of(from_a, 1)[:, :, None]]
    all_to_all x1 -> x0, starting transfers between devices: 4.03 us -> none  [shards(): lax.all_to_all(outgoing, 'bx', split_axis=0, concat_axis=0, tiled=True)]
  transfers between devices with their start and end apart: 7 -> 0, of which waited for: 4 -> 0; matrix products, arithmetic and copies ran while one was open for 7% -> 0% of each run, Pallas kernels for 0% -> 0%
where the time goes in v1:
time: 38.8 us; the launch traced here: 38.5 us
  Pallas kernels  32.1 us (83%)
  local copies, waits for them, and re-layouts  5.81 us (15%)
  between operations  0.65 us (2%)
    pallas_call x1, Pallas kernels, shards(): pl.pallas_call(functools.partial(kernel, columns, most), out_shape=(jax.S...  32.1 us
    unnamed x12, local copies, waits for them, and re-layouts  5.81 us

profile of v1, /device:TPU:0, one launch (start us, length us, event | category | flops | bytes accessed | tf_op | source)
XLA Modules:
  0.0 38.5 jit_solution(15216849018725548569)
XLA Ops:
  0.6 0.0 copy-start
  0.6 1.6 %copy-done = bf16[1,1,64,128,128]{4,3,2,1,0:T(8,128)(2,1)S(1)} copy-done((bf16[1,1,64,128,128]{4,3,2,1,0:T(8,128)(2,1)S(1)}, bf16[1,1,64,128,128]{4,3,2,1,0:T(8,128)(2,1)}, u32[]{:S(2)}) %copy-start) | copy-done | bytes 2097176
  2.2 0.0 copy-start.1
  2.2 0.9 %copy-done.1 = bf16[8,128,128]{2,1,0:T(8,128)(2,1)S(1)} copy-done((bf16[8,128,128]{2,1,0:T(8,128)(2,1)S(1)}, bf16[8,128,128]{2,1,0:T(8,128)(2,1)}, u32[]{:S(2)}) %copy-start.1) | copy-done | bytes 262168
  3.2 0.0 copy-start.2
  3.2 0.7 %copy-done.2 = f32[1,1,16,256]{3,2,1,0:T(8,128)S(1)} copy-done((f32[1,1,16,256]{3,2,1,0:T(8,128)S(1)}, f32[1,1,16,256]{3,2,1,0:T(8,128)}, u32[]{:S(2)}) %copy-start.2) | copy-done | bytes 16408
  3.9 0.0 copy-start.3
  3.9 0.7 %copy-done.3 = s32[1,4,64]{2,1,0:T(4,128)S(1)} copy-done((s32[1,4,64]{2,1,0:T(4,128)S(1)}, s32[1,4,64]{2,1,0:T(4,128)}, u32[]{:S(2)}) %copy-start.3) | copy-done | bytes 1048
  4.6 0.0 copy-start.4
  4.6 0.7 %copy-done.4 = s32[1,1,64,1]{2,3,1,0:T(1,128)S(1)} copy-done((s32[1,1,64,1]{2,3,1,0:T(1,128)S(1)}, s32[1,1,64,1]{2,3,1,0:T(1,128)}, u32[]{:S(2)}) %copy-start.4) | copy-done | bytes 280
  5.2 32.1 %shard_map.68 = (f32[16,256]{1,0:T(8,128)S(1)}, f32[4,24,128]{2,1,0:T(8,128)S(1)}) custom-call(s32[4,64]{1,0:T(4,128)S(1)} %bitcast.10, bf16[64,128,128]{2,1,0:T(8,128)(2,1)S(1)} %bitcast.6, bf16[8,128,128]{2,1,0:T(8,128)(2,1)S(1)} %copy-done.1, s32[1,64]{1,0:T(1,128)S(1)} %bitcast.11, f32[16,256]{1,0:T(8,128)S(1)} %bitcast.8), custom_call_target="tpu_custom_call" | custom-call | tf_op jit(solution)/shard_map/pallas_call | solution.py:428
  37.3 0.6 %copy.9 = f32[1,1,16,256]{3,2,1,0:T(8,128)} copy(f32[1,1,16,256]{3,2,1,0:T(8,128)S(1)} %bitcast.9) | data formatting | bytes 32768
  37.9 0.6 %copy.10 = f32[1,1,4,24,128]{4,3,2,1,0:T(8,128)} copy(f32[1,1,4,24,128]{4,3,2,1,0:T(8,128)S(1)} %bitcast.7) | data formatting | bytes 98304
Async XLA Ops:
  0.6 1.6 %copy-start = (bf16[1,1,64,128,128]{4,3,2,1,0:T(8,128)(2,1)S(1)}, bf16[1,1,64,128,128]{4,3,2,1,0:T(8,128)(2,1)}, u32[]{:S(2)}) copy-start(bf16[1,1,64,128,128]{4,3,2,1,0:T(8,128)(2,1)} %param.5) | copy-start | bytes 6291460
  2.2 0.9 %copy-start.1 = (bf16[8,128,128]{2,1,0:T(8,128)(2,1)S(1)}, bf16[8,128,128]{2,1,0:T(8,128)(2,1)}, u32[]{:S(2)}) copy-start(bf16[8,128,128]{2,1,0:T(8,128)(2,1)} %maps_ref.1) | copy-start | bytes 786436
  3.2 0.7 %copy-start.2 = (f32[1,1,16,256]{3,2,1,0:T(8,128)S(1)}, f32[1,1,16,256]{3,2,1,0:T(8,128)}, u32[]{:S(2)}) copy-start(f32[1,1,16,256]{3,2,1,0:T(8,128)} %param.9) | copy-start | bytes 49156
  3.9 0.7 %copy-start.3 = (s32[1,4,64]{2,1,0:T(4,128)S(1)}, s32[1,4,64]{2,1,0:T(4,128)}, u32[]{:S(2)}) copy-start(s32[1,4,64]{2,1,0:T(4,128)} %param.7) | copy-start | bytes 3076
  4.6 0.7 %copy-start.4 = (s32[1,1,64,1]{2,3,1,0:T(1,128)S(1)}, s32[1,1,64,1]{2,3,1,0:T(1,128)}, u32[]{:S(2)}) copy-start(s32[1,1,64,1]{2,3,1,0:T(1,128)} %param.8) | copy-start | bytes 772

commit v2 on v1

--- a/solution.py
+++ b/solution.py
@@ -10,6 +10,7 @@
 MESH = pl.DeviceIdType.MESH
 F32 = jnp.float32
 BF16 = jnp.bfloat16
+GROUP = 8
 
 
 def halves(value):
@@ -30,13 +31,17 @@
 def kernel(
     columns,
     most,
+    classes_hbm,
+    factor_ref,
+    maps_hbm,
+    owners_hbm,
+    top_hbm,
+    out_ref,
+    delivered_ref,
     classes_ref,
-    factor_ref,
     maps_ref,
     owners_ref,
     top_ref,
-    out_ref,
-    delivered_ref,
     factors,
     leaf_maps,
     inward,
@@ -51,9 +56,11 @@
     leaves,
     home,
     outgoing,
-    arrived,
     outs,
     outs_out,
+    result,
+    operand_sem,
+    result_sem,
     local_sem,
     factor_send,
     factor_recv,
@@ -71,6 +78,8 @@
     face = leaf // 4
     half, quarter = leaves_here // 2, leaves_here // 4
     pairs = quarter // 2
+    per_stage = quarter // GROUP
+    turns = 2 * per_stage
     row, column = lax.axis_index("by"), lax.axis_index("bx")
     rp, cp = lax.rem(row, 2), lax.rem(column, 2)
     row_mate, column_mate = row + 1 - 2 * rp, column + 1 - 2 * cp
@@ -89,19 +98,33 @@
             device_id={"bx": column_mate}, device_id_type=MESH,
         )
 
+    operands = [
+        pltpu.make_async_copy(source, target, operand_sem.at[index])
+        for index, (source, target) in enumerate(
+            (
+                (top_hbm, top_ref),
+                (classes_hbm, classes_ref),
+                (maps_hbm, maps_ref),
+                (owners_hbm, owners_ref),
+            )
+        )
+    ]
+    for copy in operands:
+        copy.start()
     own_copies, mate_copies = [], []
-    for index, begin in enumerate((first, second)):
+    begins = [start + GROUP * index for start in (first, second) for index in range(per_stage)]
+    for index, begin in enumerate(begins):
         own = pltpu.make_async_copy(
-            factor_ref.at[pl.ds(rp * half + begin, quarter)],
-            factors.at[rp, pl.ds(begin, quarter)],
+            factor_ref.at[pl.ds(rp * half + begin, GROUP)],
+            factors.at[rp, pl.ds(begin, GROUP)],
             local_sem.at[index],
         )
         own.start()
         own_copies.append(own)
         mate_copies.append(
             to_row_mate(
-                factor_ref.at[pl.ds((1 - rp) * half + begin, quarter)],
-                factors.at[rp, pl.ds(begin, quarter)],
+                factor_ref.at[pl.ds((1 - rp) * half + begin, GROUP)],
+                factors.at[rp, pl.ds(begin, GROUP)],
                 factor_send.at[index],
                 factor_recv.at[index],
             )
@@ -117,6 +140,7 @@
     for copy in mate_copies:
         copy.start()
 
+    operands[0].wait()
     top = top_ref[...]
     none = jnp.zeros((quarter, face), F32)
 
@@ -148,8 +172,8 @@
 
     def block_copy(step):
         return to_column_mate(
-            blocks.at[0, pl.ds(2 * step, 2)],
-            blocks.at[1 + cp, pl.ds(2 * step, 2)],
+            blocks.at[0, pl.ds(step * (GROUP // 2), GROUP // 2)],
+            blocks.at[1 + cp, pl.ds(step * (GROUP // 2), GROUP // 2)],
             block_send.at[step],
             block_recv.at[step],
         )
@@ -158,24 +182,17 @@
         return jnp.where(west, matrix[face : 2 * face], matrix[:face])
 
     def upward(turn, carry):
-        stage, step = turn // 4, lax.rem(turn, 4)
-        side = jnp.where(turn < 4, 1 - cp, cp)
-
-        @pl.when(step == 0)
-        def _():
-            @pl.when(stage == 0)
+        stage, step = turn // per_stage, lax.rem(turn, per_stage)
+        side = jnp.where(stage == 0, 1 - cp, cp)
+        slot = jnp.where(stage == 0, 0, 1 + cp)
+        for index in range(turns):
+
+            @pl.when(turn == index)
             def _():
-                own_copies[0].wait()
-                mate_copies[0].wait_recv()
-                field_copy.wait_recv()
-
-            @pl.when(stage == 1)
-            def _():
-                own_copies[1].wait()
-                mate_copies[1].wait_recv()
-
-        slot = jnp.where(turn < 4, 0, 1 + cp)
-        boxes = [2 * step, 2 * step + 1, 2 * step + pairs, 2 * step + 1 + pairs]
+                own_copies[index].wait()
+                mate_copies[index].wait_recv()
+
+        boxes = [step * GROUP + index for index in range(GROUP)]
         places = [side * quarter + box for box in boxes]
         maps_a, maps_b = [], []
         for place in places:
@@ -189,31 +206,37 @@
             maps_b.append(map_b)
         rows_a = [m[3 * face :] for m in maps_a]
         rows_b = [m[2 * face : 3 * face] for m in maps_b]
-        a_ss = [m[:, 3 * face :] for m in rows_a]
-        b_ss = [m[:, 2 * face : 3 * face] for m in rows_b]
-        crossed_rows = [product(b, a) for b, a in zip(b_ss, rows_a)]
-        crossed = [m[:, 3 * face :] for m in crossed_rows]
-        squares = [product(m, m) for m in crossed]
-        inverses = [product(identity + m, identity + s) for m, s in zip(crossed, squares)]
-        inward_a = [
-            product(w, jnp.concatenate([c, -b], axis=1))
-            for w, c, b in zip(inverses, crossed_rows, rows_b)
-        ]
         inner_a = [inner_rows(m) for m in maps_a]
         inner_b = [inner_rows(m) for m in maps_b]
-        spread = [
-            product(jnp.concatenate([s, i[:, 3 * face :]], axis=0), x)
-            for s, i, x in zip(a_ss, inner_a, inward_a)
+        firsts = [
+            product(jnp.concatenate([b, i], axis=0)[:, 2 * face : 3 * face], a)
+            for b, i, a in zip(rows_b, inner_b, rows_a)
         ]
+        starts = [jnp.concatenate([f[:face], -b], axis=1) for f, b in zip(firsts, rows_b)]
+        lefts = [
+            jnp.concatenate([f[:face], a, i, f[face:]], axis=0)[:, 3 * face :]
+            for f, a, i in zip(firsts, rows_a, inner_a)
+        ]
+        seconds = [product(left, left[:face]) for left in lefts]
+        rights = [st + product(sec[:face], st) for st, sec in zip(starts, seconds)]
+        spreads = [
+            product(
+                jnp.concatenate([identity + left[:face], left[face:] + sec[face:]], axis=0), right
+            )
+            for left, sec, right in zip(lefts, seconds, rights)
+        ]
+        inward_a = [sp[:face] for sp in spreads]
         inward_b = [
-            -jnp.concatenate([a, no_map], axis=1) - s[:face] for a, s in zip(rows_a, spread)
+            -jnp.concatenate([a, no_map], axis=1) - sp[face : 2 * face]
+            for a, sp in zip(rows_a, spreads)
         ]
         upper = [
-            jnp.concatenate([i, no_map], axis=1) + s[face:] for i, s in zip(inner_a, spread)
+            jnp.concatenate([i, no_map], axis=1) + sp[2 * face : 3 * face]
+            for i, sp in zip(inner_a, spreads)
         ]
         lower = [
-            jnp.concatenate([no_map, i], axis=1) + product(i[:, 2 * face : 3 * face], y)
-            for i, y in zip(inner_b, inward_b)
+            jnp.concatenate([-f[face:], i], axis=1) - sp[3 * face :]
+            for f, i, sp in zip(firsts, inner_b, spreads)
         ]
         packed = []
         for index, (box, place) in enumerate(zip(boxes, places)):
@@ -227,14 +250,14 @@
             answers[slot, box] = jnp.sum(
                 jnp.where(sub_two == lane_two, answer, 0.0), axis=0, keepdims=True
             )
-            offset = 2 * face * (index // 2)
+            offset = 2 * face * (index % 2)
             shift = offset - face * (1 - cp) + leaf
             moved_a = pltpu.roll(level[:, :leaf], lax.rem(shift, leaf), 1)
             moved_b = pltpu.roll(level[:, leaf:], lax.rem(shift + face, leaf), 1)
             packed.append(jnp.where(lane_two < offset + face, moved_a, moved_b))
-        for index in range(2):
-            blocks[slot, 2 * step + index] = jnp.where(
-                lane_two < 2 * face, packed[index], packed[index + 2]
+        for index in range(GROUP // 2):
+            blocks[slot, step * (GROUP // 2) + index] = jnp.where(
+                lane_two < 2 * face, packed[2 * index], packed[2 * index + 1]
             )
 
         @pl.when(stage == 0)
@@ -243,12 +266,16 @@
 
         return carry
 
-    lax.fori_loop(0, 8, upward, 0)
+    operands[1].wait()
+    operands[2].wait()
+    field_copy.wait_recv()
+    lax.fori_loop(0, turns, upward, 0)
     answer_copy = to_column_mate(
         answers.at[0], answers.at[1 + cp], answer_sem.at[0], answer_sem.at[1]
     )
     answer_copy.start()
 
+    operands[3].wait()
     target = owners_ref[...]
     named = (lax.broadcasted_iota(jnp.int32, (columns, leaves_here), 0) == target).astype(F32)
     before = lax.broadcasted_iota(jnp.int32, (leaves_here, leaves_here), 0) < (
@@ -262,16 +289,16 @@
     wanted = lax.broadcasted_iota(jnp.int32, (columns * most, leaves_here), 0).astype(F32)
     selector = (wanted == slots).astype(F32).astype(BF16)
 
-    for step in range(4):
+    for step in range(per_stage):
         block_copy(step).wait_recv()
     answer_copy.wait_recv()
     for index in range(pairs):
         both = blocks[1, index].T
-        transposed[index] = both[: 2 * face]
-        transposed[index + pairs] = both[2 * face :]
+        transposed[2 * index] = both[: 2 * face]
+        transposed[2 * index + 1] = both[2 * face :]
         other = blocks[2, index]
-        opened[index] = other[:, : 2 * face]
-        opened[index + pairs] = other[:, 2 * face :]
+        opened[2 * index] = other[:, : 2 * face]
+        opened[2 * index + 1] = other[:, 2 * face :]
     diagonal = (
         lax.broadcasted_iota(jnp.int32, (quarter, 2 * face, 2 * face), 1)
         == lax.broadcasted_iota(jnp.int32, (quarter, 2 * face, 2 * face), 2)
@@ -381,7 +408,7 @@
         owner = lax.rem(column + step, columns)
         copy = pltpu.make_async_remote_copy(
             src_ref=outgoing.at[owner],
-            dst_ref=arrived.at[column],
+            dst_ref=delivered_ref.at[column],
             send_sem=all_send.at[step - 1],
             recv_sem=all_recv.at[step - 1],
             device_id={"bx": owner},
@@ -389,12 +416,15 @@
         )
         copy.start()
         all_copies.append(copy)
-    arrived[column] = outgoing[column]
+    keep = pltpu.make_async_copy(
+        outgoing.at[column], delivered_ref.at[column], result_sem.at[0]
+    )
+    keep.start()
 
     outward(cp, outs.at[cp])
     outs_copy.wait_recv()
     out_west, out_east = outs[0], outs[1]
-    out_ref[...] = jnp.concatenate(
+    result[...] = jnp.concatenate(
         [
             out_west[:, : 2 * face],
             out_east[:, : 2 * face],
@@ -405,15 +435,18 @@
         ],
         axis=1,
     )
+    result_copy = pltpu.make_async_copy(result, out_ref, result_sem.at[1])
+    result_copy.start()
     for copy in all_copies:
         copy.wait_recv()
-    delivered_ref[...] = arrived[...]
+    keep.wait()
+    result_copy.wait()
 
     for copy in mate_copies + all_copies:
         copy.wait_send()
     for copy in (field_copy, answer_copy, inner_copy, leaf_copy, outs_copy):
         copy.wait_send()
-    for step in range(4):
+    for step in range(per_stage):
         block_copy(step).wait_send()
 
 
@@ -424,22 +457,20 @@
     inside = leaf // 2
     columns = lax.axis_size("bx")
     most = max(2, (3 * leaves_here + 2 * columns - 1) // (2 * columns))
-    whole = pl.BlockSpec(memory_space=pltpu.VMEM)
+    whole = pl.BlockSpec(memory_space=pl.ANY)
     top_out, arrived = pl.pallas_call(
         functools.partial(kernel, columns, most),
         out_shape=(
             jax.ShapeDtypeStruct((quarter, 2 * leaf), F32),
             jax.ShapeDtypeStruct((columns, most, leaf), F32),
         ),
-        in_specs=[
-            pl.BlockSpec(memory_space=pltpu.SMEM),
-            pl.BlockSpec(memory_space=pl.ANY),
-            whole,
-            whole,
-            whole,
-        ],
+        in_specs=[whole] * 5,
         out_specs=(whole, whole),
         scratch_shapes=[
+            pltpu.SMEM(depth_class.shape[1:], jnp.int32),
+            pltpu.VMEM(class_maps.shape, BF16),
+            pltpu.VMEM((1, leaves_here), jnp.int32),
+            pltpu.VMEM((quarter, 2 * leaf), F32),
             pltpu.VMEM((2, half, leaf, leaf), BF16),
             pltpu.VMEM((2, half, leaf, leaf), F32),
             pltpu.VMEM((half, inside, 2 * leaf), F32),
@@ -454,15 +485,17 @@
             pltpu.VMEM((2, half, leaf), F32),
             pltpu.VMEM((2, half, leaf), F32),
             pltpu.VMEM((columns, most, leaf), F32),
-            pltpu.VMEM((columns, most, leaf), F32),
             pltpu.VMEM((2, quarter, leaf), F32),
             pltpu.VMEM((quarter, leaf), F32),
+            pltpu.VMEM((quarter, 2 * leaf), F32),
+            pltpu.SemaphoreType.DMA((4,)),
             pltpu.SemaphoreType.DMA((2,)),
+            pltpu.SemaphoreType.DMA((half // GROUP,)),
+            pltpu.SemaphoreType.DMA((half // GROUP,)),
+            pltpu.SemaphoreType.DMA((half // GROUP,)),
             pltpu.SemaphoreType.DMA((2,)),
-            pltpu.SemaphoreType.DMA((2,)),
-            pltpu.SemaphoreType.DMA((2,)),
-            pltpu.SemaphoreType.DMA((4,)),
-            pltpu.SemaphoreType.DMA((4,)),
+            pltpu.SemaphoreType.DMA((quarter // GROUP,)),
+            pltpu.SemaphoreType.DMA((quarter // GROUP,)),
             pltpu.SemaphoreType.DMA((2,)),
             pltpu.SemaphoreType.DMA((2,)),
             pltpu.SemaphoreType.DMA((2,)),

time: 38.8 us -> 32.9 us (0.85)
  Pallas kernels: 32.1 us -> 26.2 us
    pallas_call x1, Pallas kernels: 32.1 us -> 26.2 us  [shards(): pl.pallas_call(functools.partial(kernel, columns, most), out_shape=(jax.S...]
where the time goes in v2:
time: 32.9 us; the launch traced here: 32.7 us
  Pallas kernels  26.2 us (80%)
  local copies, waits for them, and re-layouts  5.81 us (18%)
  between operations  0.65 us (2%)
    pallas_call x1, Pallas kernels, shards(): pl.pallas_call(functools.partial(kernel, columns, most), out_shape=(jax.S...  26.2 us
    unnamed x12, local copies, waits for them, and re-layouts  5.81 us

profile of v2, /device:TPU:0, one launch (start us, length us, event | category | flops | bytes accessed | tf_op | source)
XLA Modules:
  0.0 32.7 jit_solution(7573064076833747430)
XLA Ops:
  0.6 0.0 copy-start
  0.6 1.6 %copy-done = bf16[1,1,64,128,128]{4,3,2,1,0:T(8,128)(2,1)S(1)} copy-done((bf16[1,1,64,128,128]{4,3,2,1,0:T(8,128)(2,1)S(1)}, bf16[1,1,64,128,128]{4,3,2,1,0:T(8,128)(2,1)}, u32[]{:S(2)}) %copy-start) | copy-done | bytes 2097176
  2.2 0.0 copy-start.1
  2.2 0.9 %copy-done.1 = bf16[8,128,128]{2,1,0:T(8,128)(2,1)S(1)} copy-done((bf16[8,128,128]{2,1,0:T(8,128)(2,1)S(1)}, bf16[8,128,128]{2,1,0:T(8,128)(2,1)}, u32[]{:S(2)}) %copy-start.1) | copy-done | bytes 262168
  3.2 0.0 copy-start.2
  3.2 0.7 %copy-done.2 = f32[1,1,16,256]{3,2,1,0:T(8,128)S(1)} copy-done((f32[1,1,16,256]{3,2,1,0:T(8,128)S(1)}, f32[1,1,16,256]{3,2,1,0:T(8,128)}, u32[]{:S(2)}) %copy-start.2) | copy-done | bytes 16408
  3.9 0.0 copy-start.3
  3.9 0.7 %copy-done.3 = s32[1,4,64]{2,1,0:T(4,128)S(1)} copy-done((s32[1,4,64]{2,1,0:T(4,128)S(1)}, s32[1,4,64]{2,1,0:T(4,128)}, u32[]{:S(2)}) %copy-start.3) | copy-done | bytes 1048
  4.6 0.0 copy-start.4
  4.6 0.7 %copy-done.4 = s32[1,1,64,1]{2,3,1,0:T(1,128)S(1)} copy-done((s32[1,1,64,1]{2,3,1,0:T(1,128)S(1)}, s32[1,1,64,1]{2,3,1,0:T(1,128)}, u32[]{:S(2)}) %copy-start.4) | copy-done | bytes 280
  5.2 26.2 %shard_map.68 = (f32[16,256]{1,0:T(8,128)S(1)}, f32[4,24,128]{2,1,0:T(8,128)S(1)}) custom-call(s32[4,64]{1,0:T(4,128)S(1)} %bitcast.10, bf16[64,128,128]{2,1,0:T(8,128)(2,1)S(1)} %bitcast.6, bf16[8,128,128]{2,1,0:T(8,128)(2,1)S(1)} %copy-done.1, s32[1,64]{1,0:T(1,128)S(1)} %bitcast.11, f32[16,256]{1,0:T(8,128)S(1)} %bitcast.8), custom_call_target="tpu_custom_call" | custom-call | tf_op jit(solution)/shard_map/pallas_call | solution.py:461
  31.5 0.6 %copy.9 = f32[1,1,16,256]{3,2,1,0:T(8,128)} copy(f32[1,1,16,256]{3,2,1,0:T(8,128)S(1)} %bitcast.9) | data formatting | bytes 32768
  32.1 0.6 %copy.10 = f32[1,1,4,24,128]{4,3,2,1,0:T(8,128)} copy(f32[1,1,4,24,128]{4,3,2,1,0:T(8,128)S(1)} %bitcast.7) | data formatting | bytes 98304
Async XLA Ops:
  0.6 1.6 %copy-start = (bf16[1,1,64,128,128]{4,3,2,1,0:T(8,128)(2,1)S(1)}, bf16[1,1,64,128,128]{4,3,2,1,0:T(8,128)(2,1)}, u32[]{:S(2)}) copy-start(bf16[1,1,64,128,128]{4,3,2,1,0:T(8,128)(2,1)} %param.5) | copy-start | bytes 6291460
  2.2 0.9 %copy-start.1 = (bf16[8,128,128]{2,1,0:T(8,128)(2,1)S(1)}, bf16[8,128,128]{2,1,0:T(8,128)(2,1)}, u32[]{:S(2)}) copy-start(bf16[8,128,128]{2,1,0:T(8,128)(2,1)} %maps_hbm.1) | copy-start | bytes 786436
  3.2 0.7 %copy-start.2 = (f32[1,1,16,256]{3,2,1,0:T(8,128)S(1)}, f32[1,1,16,256]{3,2,1,0:T(8,128)}, u32[]{:S(2)}) copy-start(f32[1,1,16,256]{3,2,1,0:T(8,128)} %param.9) | copy-start | bytes 49156
  3.9 0.7 %copy-start.3 = (s32[1,4,64]{2,1,0:T(4,128)S(1)}, s32[1,4,64]{2,1,0:T(4,128)}, u32[]{:S(2)}) copy-start(s32[1,4,64]{2,1,0:T(4,128)} %param.7) | copy-start | bytes 3076
  4.6 0.7 %copy-start.4 = (s32[1,1,64,1]{2,3,1,0:T(1,128)S(1)}, s32[1,1,64,1]{2,3,1,0:T(1,128)}, u32[]{:S(2)}) copy-start(s32[1,1,64,1]{2,3,1,0:T(1,128)} %param.8) | copy-start | bytes 772

commit v3 on v2

--- a/solution.py
+++ b/solution.py
@@ -11,6 +11,7 @@
 F32 = jnp.float32
 BF16 = jnp.bfloat16
 GROUP = 8
+LEVELS = 32767.0
 
 
 def halves(value):
@@ -25,6 +26,13 @@
         jnp.concatenate([left_high, left_high, left_low], axis=1),
         jnp.concatenate([right_high, right_low, right_high], axis=0),
         preferred_element_type=F32,
+    )
+
+
+def lane_sums(values):
+    ones = jnp.ones((2 * values.shape[1], values.shape[1]), BF16)
+    return jnp.dot(
+        jnp.concatenate(halves(values), axis=1), ones, preferred_element_type=F32
     )
 
 
@@ -45,7 +53,10 @@
     factors,
     leaf_maps,
     inward,
+    levels,
     blocks,
+    coded,
+    coded_in,
     answers,
     fields,
     fields_out,
@@ -172,14 +183,20 @@
 
     def block_copy(step):
         return to_column_mate(
-            blocks.at[0, pl.ds(step * (GROUP // 2), GROUP // 2)],
-            blocks.at[1 + cp, pl.ds(step * (GROUP // 2), GROUP // 2)],
+            coded.at[0, pl.ds(step * (GROUP // 2), GROUP // 2)],
+            coded_in.at[pl.ds(step * (GROUP // 2), GROUP // 2)],
             block_send.at[step],
             block_recv.at[step],
         )
 
     def inner_rows(matrix):
         return jnp.where(west, matrix[face : 2 * face], matrix[:face])
+
+    picker_row = lax.broadcasted_iota(jnp.int32, (8 * leaf, leaf), 0)
+    picker_lane = lax.broadcasted_iota(jnp.int32, (8 * leaf, leaf), 1)
+    piece, source = picker_row // leaf, lax.rem(picker_row, leaf) - face * (1 - cp)
+    spot = 2 * face * (piece // 4) + face * (lax.rem(piece, 2)) + source
+    picker = jnp.where((source >= 0) & (source < face) & (picker_lane == spot), 1.0, 0.0).astype(BF16)
 
     def upward(turn, carry):
         stage, step = turn // per_stage, lax.rem(turn, per_stage)
@@ -238,27 +255,32 @@
             jnp.concatenate([-f[face:], i], axis=1) - sp[3 * face :]
             for f, i, sp in zip(firsts, inner_b, spreads)
         ]
-        packed = []
-        for index, (box, place) in enumerate(zip(boxes, places)):
+        pieces = []
+        for index, place in enumerate(places):
             inward[place, :face] = inward_a[index]
             inward[place, face:] = inward_b[index]
             level = jnp.concatenate([upper[index], lower[index]], axis=0)
-            field_a, field_b = fields[side, 0, box], fields[side, 1, box]
-            answer = jnp.sum(
-                level[:, :leaf] * field_a + level[:, leaf:] * field_b, axis=1, keepdims=True
-            )
-            answers[slot, box] = jnp.sum(
-                jnp.where(sub_two == lane_two, answer, 0.0), axis=0, keepdims=True
-            )
-            offset = 2 * face * (index % 2)
-            shift = offset - face * (1 - cp) + leaf
-            moved_a = pltpu.roll(level[:, :leaf], lax.rem(shift, leaf), 1)
-            moved_b = pltpu.roll(level[:, leaf:], lax.rem(shift + face, leaf), 1)
-            packed.append(jnp.where(lane_two < offset + face, moved_a, moved_b))
+            levels[place] = level
+            pieces.append(jnp.concatenate(halves(level), axis=1))
+        packed = jnp.dot(
+            jnp.concatenate(
+                [
+                    jnp.concatenate([pieces[index], pieces[index + 1]], axis=1)
+                    for index in range(0, GROUP, 2)
+                ],
+                axis=0,
+            ),
+            picker,
+            preferred_element_type=F32,
+        )
         for index in range(GROUP // 2):
-            blocks[slot, step * (GROUP // 2) + index] = jnp.where(
-                lane_two < 2 * face, packed[2 * index], packed[2 * index + 1]
-            )
+            tile = packed[index * 2 * face : (index + 1) * 2 * face]
+            pair = step * (GROUP // 2) + index
+            blocks[stage, pair] = tile
+            scale = jnp.maximum(jnp.max(jnp.abs(tile), axis=0, keepdims=True), 1e-30)
+            code = jnp.round(tile * (LEVELS / scale))
+            coded[stage, pair] = code.astype(jnp.int32).astype(jnp.int16)
+            answers[slot, quarter + pair] = scale * (1.0 / LEVELS)
 
         @pl.when(stage == 0)
         def _():
@@ -268,12 +290,37 @@
 
     operands[1].wait()
     operands[2].wait()
+    lax.fori_loop(0, turns, upward, 0)
+
+    def answer(turn, carry):
+        stage, step = turn // per_stage, lax.rem(turn, per_stage)
+        side = jnp.where(stage == 0, 1 - cp, cp)
+        slot = jnp.where(stage == 0, 0, 1 + cp)
+        parts = []
+        for index in range(GROUP):
+            box = step * GROUP + index
+            level = levels[side * quarter + box]
+            parts.append(
+                level[:, :leaf] * fields[side, 0, box] + level[:, leaf:] * fields[side, 1, box]
+            )
+        sums = lane_sums(jnp.concatenate(parts, axis=0))
+        for index in range(GROUP):
+            answers[slot, step * GROUP + index] = jnp.sum(
+                jnp.where(
+                    sub_two == lane_two, sums[index * 2 * face : (index + 1) * 2 * face], 0.0
+                ),
+                axis=0,
+                keepdims=True,
+            )
+        return carry
+
     field_copy.wait_recv()
-    lax.fori_loop(0, turns, upward, 0)
+    lax.fori_loop(0, per_stage, answer, 0)
     answer_copy = to_column_mate(
         answers.at[0], answers.at[1 + cp], answer_sem.at[0], answer_sem.at[1]
     )
     answer_copy.start()
+    lax.fori_loop(per_stage, turns, answer, 0)
 
     operands[3].wait()
     target = owners_ref[...]
@@ -293,18 +340,21 @@
         block_copy(step).wait_recv()
     answer_copy.wait_recv()
     for index in range(pairs):
-        both = blocks[1, index].T
+        mine = blocks[1, index]
+        received = coded_in[index].astype(jnp.int32).astype(F32)
+        received = received * answers[2 - cp, quarter + index]
+        both = jnp.where(west, mine, received).T
         transposed[2 * index] = both[: 2 * face]
         transposed[2 * index + 1] = both[2 * face :]
-        other = blocks[2, index]
+        other = jnp.where(west, received, mine)
         opened[2 * index] = other[:, : 2 * face]
         opened[2 * index + 1] = other[:, 2 * face :]
     diagonal = (
         lax.broadcasted_iota(jnp.int32, (quarter, 2 * face, 2 * face), 1)
         == lax.broadcasted_iota(jnp.int32, (quarter, 2 * face, 2 * face), 2)
     )
-    west_out = answers[1][:, :, : 2 * face]
-    east_out = answers[2][:, :, : 2 * face]
+    west_out = answers[1][:quarter, :, : 2 * face]
+    east_out = answers[2][:quarter, :, : 2 * face]
     start = jnp.sum(
         opened[...] * west_out - jnp.where(diagonal, east_out, 0.0), axis=2, keepdims=True
     )
@@ -334,28 +384,29 @@
     lane_row = lax.broadcasted_iota(jnp.int32, (face, leaf), 1)
 
     def downward(turn, carry):
-        side = jnp.where(turn < 4, cp, 1 - cp)
-
-        @pl.when(turn == 4)
-        def _():
-            inner_copy.wait_recv()
-
-        for index in range(4):
-            box = lax.rem(turn, 4) * 4 + index
-            place = side * quarter + box
+        stage, step = turn // per_stage, lax.rem(turn, per_stage)
+        side = jnp.where(stage == 0, cp, 1 - cp)
+        parts, known = [], []
+        for index in range(GROUP):
+            box = step * GROUP + index
             field_a = fields[side, 0, box] + inner[side, 0, box]
             field_b = fields[side, 1, box] + inner[side, 1, box]
-            both = inward[place]
-            found = jnp.sum(
-                both[:, :leaf] * field_a + both[:, leaf:] * field_b, axis=1, keepdims=True
-            )
+            both = inward[side * quarter + box]
+            parts.append(both[:, :leaf] * field_a + both[:, leaf:] * field_b)
+            known.append((field_a, field_b))
+        sums = lane_sums(jnp.concatenate(parts, axis=0))
+        for index in range(GROUP):
+            place = side * quarter + step * GROUP + index
+            found = sums[index * 2 * face : (index + 1) * 2 * face]
             north = jnp.where(lane_row == sub_row + 3 * face, found[:face], 0.0)
             south = jnp.where(lane_row == sub_row + 2 * face, found[face:], 0.0)
-            leaves[0, pl.ds(place, 1)] = field_a + jnp.sum(north, axis=0, keepdims=True)
-            leaves[1, pl.ds(place, 1)] = field_b + jnp.sum(south, axis=0, keepdims=True)
+            leaves[0, pl.ds(place, 1)] = known[index][0] + jnp.sum(north, axis=0, keepdims=True)
+            leaves[1, pl.ds(place, 1)] = known[index][1] + jnp.sum(south, axis=0, keepdims=True)
         return carry
 
-    lax.fori_loop(0, 8, downward, 0)
+    lax.fori_loop(0, per_stage, downward, 0)
+    inner_copy.wait_recv()
+    lax.fori_loop(per_stage, turns, downward, 0)
     leaf_copy = to_row_mate(leaves.at[1 - rp], home.at[rp], leaf_sem.at[0], leaf_sem.at[1])
     leaf_copy.start()
     home[rp] = leaves[rp]
@@ -365,28 +416,30 @@
 
     def outward(side, target_ref):
         def body(turn, carry):
-            for index in range(4):
-                box = turn * 4 + index
-                place = side * quarter + box
+            parts = []
+            for index in range(GROUP):
+                place = side * quarter + turn * GROUP + index
                 leaf_a = leaves[0, pl.ds(place, 1)]
                 leaf_b = leaves[1, pl.ds(place, 1)]
                 outer = pl.ds(cp * face, face)
-                found = jnp.concatenate(
-                    [
-                        leaf_maps[0, place, outer] * leaf_a,
-                        leaf_maps[1, place, outer] * leaf_b,
-                        leaf_maps[0, place, 2 * face : 3 * face] * leaf_a,
-                        leaf_maps[1, place, 3 * face :] * leaf_b,
-                    ],
+                parts += [
+                    leaf_maps[0, place, outer] * leaf_a,
+                    leaf_maps[1, place, outer] * leaf_b,
+                    leaf_maps[0, place, 2 * face : 3 * face] * leaf_a,
+                    leaf_maps[1, place, 3 * face :] * leaf_b,
+                ]
+            sums = lane_sums(jnp.concatenate(parts, axis=0))
+            for index in range(GROUP):
+                target_ref[pl.ds(turn * GROUP + index, 1)] = jnp.sum(
+                    jnp.where(
+                        sub_all == lane_all, sums[index * leaf : (index + 1) * leaf], 0.0
+                    ),
                     axis=0,
-                )
-                found = jnp.sum(found, axis=1, keepdims=True)
-                target_ref[pl.ds(box, 1)] = jnp.sum(
-                    jnp.where(sub_all == lane_all, found, 0.0), axis=0, keepdims=True
+                    keepdims=True,
                 )
             return carry
 
-        lax.fori_loop(0, quarter // 4, body, 0)
+        lax.fori_loop(0, per_stage, body, 0)
 
     outward(1 - cp, outs_out)
     outs_copy = to_column_mate(outs_out, outs.at[cp], outs_sem.at[0], outs_sem.at[1])
@@ -474,8 +527,11 @@
             pltpu.VMEM((2, half, leaf, leaf), BF16),
             pltpu.VMEM((2, half, leaf, leaf), F32),
             pltpu.VMEM((half, inside, 2 * leaf), F32),
-            pltpu.VMEM((3, quarter // 2, inside, leaf), F32),
-            pltpu.VMEM((3, quarter, 1, leaf), F32),
+            pltpu.VMEM((half, inside, 2 * leaf), F32),
+            pltpu.VMEM((2, quarter // 2, inside, leaf), F32),
+            pltpu.VMEM((2, quarter // 2, inside, leaf), jnp.int16),
+            pltpu.VMEM((quarter // 2, inside, leaf), jnp.int16),
+            pltpu.VMEM((3, quarter + quarter // 2, 1, leaf), F32),
             pltpu.VMEM((2, 2, quarter, 1, leaf), F32),
             pltpu.VMEM((2, quarter, 1, leaf), F32),
             pltpu.VMEM((quarter, inside, inside), F32),
@@ -504,7 +560,7 @@
             pltpu.SemaphoreType.DMA((columns - 1,)),
         ],
         compiler_params=pltpu.CompilerParams(
-            collective_id=0, has_side_effects=True, vmem_limit_bytes=40 * 1024 * 1024
+            collective_id=0, has_side_effects=True, vmem_limit_bytes=60 * 1024 * 1024
         ),
     )(depth_class[0], factor, class_maps, owners[0, 0].reshape(1, leaves_here), top_in[0, 0])
     return (top_out[None, None], arrived[None, None])

time: 32.9 us -> 26.9 us (0.82)
  local copies, waits for them, and re-layouts: 5.81 us -> 2.74 us
  Pallas kernels: 26.2 us -> 23.2 us
    unnamed x12 -> x2, local copies, waits for them, and re-layouts: 5.81 us -> 2.74 us
    pallas_call x1, Pallas kernels: 26.2 us -> 23.2 us  [shards(): pl.pallas_call(functools.partial(kernel, columns, most), out_shape=(jax.S...]
where the time goes in v3:
time: 26.9 us; the launch traced here: 26.6 us
  Pallas kernels  23.2 us (86%)
  local copies, waits for them, and re-layouts  2.74 us (10%)
  between operations  0.64 us (2%)
    pallas_call x1, Pallas kernels, shards(): pl.pallas_call(functools.partial(kernel, columns, most), out_shape=(jax.S...  23.2 us
    unnamed x2, local copies, waits for them, and re-layouts  2.74 us

profile of v3, /device:TPU:0, one launch (start us, length us, event | category | flops | bytes accessed | tf_op | source)
XLA Modules:
  0.0 26.6 jit_solution(1757123128692396963)
XLA Ops:
  0.6 23.2 %shard_map.68 = (f32[16,256]{1,0:T(8,128)}, f32[4,24,128]{2,1,0:T(8,128)}) custom-call(s32[4,64]{1,0:T(4,128)} %bitcast.10, bf16[64,128,128]{2,1,0:T(8,128)(2,1)} %bitcast.6, bf16[8,128,128]{2,1,0:T(8,128)(2,1)} %maps_hbm.1, s32[1,64]{1,0:T(1,128)} %bitcast.11, f32[16,256]{1,0:T(8,128)} %bitcast.8), custom_call_target="tpu_custom_call" | custom-call | tf_op jit(solution)/shard_map/pallas_call | solution.py:514
  23.9 1.3 %copy.9 = f32[1,1,16,256]{3,2,1,0:T(8,128)} copy(f32[1,1,16,256]{3,2,1,0:T(8,128)} %bitcast.9) | data formatting | bytes 32768
  25.2 1.4 %copy.10 = f32[1,1,4,24,128]{4,3,2,1,0:T(8,128)} copy(f32[1,1,4,24,128]{4,3,2,1,0:T(8,128)} %bitcast.7) | data formatting | bytes 98304

commit v4 on v3

--- a/solution.py
+++ b/solution.py
@@ -10,7 +10,7 @@
 MESH = pl.DeviceIdType.MESH
 F32 = jnp.float32
 BF16 = jnp.bfloat16
-GROUP = 8
+GROUP = 16
 LEVELS = 32767.0
 
 
@@ -503,6 +503,15 @@
         block_copy(step).wait_send()
 
 
+def relay(top_ref, rows_ref, out_ref, delivered_ref, sems):
+    first = pltpu.make_async_copy(top_ref, out_ref, sems.at[0])
+    second = pltpu.make_async_copy(rows_ref, delivered_ref, sems.at[1])
+    first.start()
+    second.start()
+    first.wait()
+    second.wait()
+
+
 def shards(leaf_factor, class_maps, depth_class, owners, top_in):
     factor = leaf_factor[0, 0]
     leaves_here, leaf = factor.shape[0], factor.shape[1]
@@ -563,6 +572,17 @@
             collective_id=0, has_side_effects=True, vmem_limit_bytes=60 * 1024 * 1024
         ),
     )(depth_class[0], factor, class_maps, owners[0, 0].reshape(1, leaves_here), top_in[0, 0])
+    near = pl.BlockSpec(memory_space=pltpu.VMEM)
+    top_out, arrived = pl.pallas_call(
+        relay,
+        out_shape=(
+            jax.ShapeDtypeStruct(top_out.shape, F32),
+            jax.ShapeDtypeStruct(arrived.shape, F32),
+        ),
+        in_specs=[near, near],
+        out_specs=(whole, whole),
+        scratch_shapes=[pltpu.SemaphoreType.DMA((2,))],
+    )(top_out, arrived)
     return (top_out[None, None], arrived[None, None])
 
 

time: 26.9 us -> 25 us (0.929)
  local copies, waits for them, and re-layouts: 2.74 us -> 0 us
  Pallas kernels: 23.2 us -> 24.1 us
    unnamed x2 -> x0, local copies, waits for them, and re-layouts: 2.74 us -> none
    pallas_call x0 -> x1, Pallas kernels: none -> 1.46 us  [shards(): pl.pallas_call(relay, out_shape=(jax.ShapeDtypeStruct(top_out.shape, F32)...]
    pallas_call x1, Pallas kernels: 23.2 us -> 22.7 us  [shards(): pl.pallas_call(functools.partial(kernel, columns, most), out_shape=(jax.S...]
where the time goes in v4:
time: 25 us; the launch traced here: 24.8 us
  Pallas kernels  24.1 us (96%)
  between operations  0.64 us (3%)
    pallas_call x1, Pallas kernels, shards(): pl.pallas_call(functools.partial(kernel, columns, most), out_shape=(jax.S...  22.7 us
    pallas_call x1, Pallas kernels, shards(): pl.pallas_call(relay, out_shape=(jax.ShapeDtypeStruct(top_out.shape, F32)...  1.46 us

profile of v4, /device:TPU:0, one launch (start us, length us, event | category | flops | bytes accessed | tf_op | source)
XLA Modules:
  0.0 24.8 jit_solution(3652662796374496133)
XLA Ops:
  0.6 22.7 %shard_map.68 = (f32[16,256]{1,0:T(8,128)}, f32[4,24,128]{2,1,0:T(8,128)}) custom-call(s32[4,64]{1,0:T(4,128)} %bitcast.8, bf16[64,128,128]{2,1,0:T(8,128)(2,1)} %bitcast.6, bf16[8,128,128]{2,1,0:T(8,128)(2,1)} %maps_hbm.1, s32[1,64]{1,0:T(1,128)} %bitcast.9, f32[16,256]{1,0:T(8,128)} %bitcast.7), custom_call_target="tpu_custom_call" | custom-call | tf_op jit(solution)/shard_map/pallas_call | solution.py:523
  23.3 1.5 %shard_map.69 = (f32[16,256]{1,0:T(8,128)}, f32[4,24,128]{2,1,0:T(8,128)}) custom-call(f32[16,256]{1,0:T(8,128)} %get-tuple-element.6.top_ref, f32[4,24,128]{2,1,0:T(8,128)} %get-tuple-element.7.rows_ref), custom_call_target="tpu_custom_call" | custom-call | tf_op jit(solution)/shard_map/pallas_call | solution.py:576
